TPU v7x, 128 devices: a whole 4x4x4 slice. The times are simulated.
128 devices in a mesh: slot: 32 (over z, x, core), grp: 4 (over y).
Axes of the slice: x: 4, y: 4, z: 4, core: 2. Of those that a mesh axis runs over, the one named last changes fastest.
Arguments:
- token_rows: bfloat16 [2, 32, 4, 384, 2048], P(None, 'slot', 'grp'), may hold values from -6 to 6
- cotangents: bfloat16 [2, 32, 4, 384, 2048], P(None, 'slot', 'grp'), may hold values from -6 to 6
- row_counts: int32 [2, 32, 4], P(None, 'slot', 'grp'), may hold values from 96 to 384, as said below
- old_place: int32 [32, 4], replicated, may hold values from 0 to 3, as said below
- new_place: int32 [32, 4], replicated, may hold values from 0 to 3, as said below
- momentum: float32 [16, 3145728], P(None, ('slot', 'grp')), may hold values from -4 to 4
- curvature: float32 [16, 3145728], P(None, ('slot', 'grp')), may hold values from 0.01 to 1
- master: float32 [16, 3145728], P(None, ('slot', 'grp')), may hold values from -0.125 to 0.125
Outputs:
- d_rows: bfloat16 [2, 32, 4, 384, 2048], P(None, 'slot', 'grp')
- momentum_out: float32 [16, 3145728], P(None, ('slot', 'grp'))
- curvature_out: float32 [16, 3145728], P(None, ('slot', 'grp'))
- master_out: float32 [16, 3145728], P(None, ('slot', 'grp'))
Inputs may be any that keep to these rules, and one draw needn't show every extreme that they name: `old_place`: entry [s, g] is the expert, numbered within group g, held by slot s of group g; each of the 4 experts of every group has at least one slot. `new_place`: entry [s, g] is the expert, numbered within group g, held by slot s of group g; each of the 4 experts of every group has at least one slot. `row_counts`: rows from this count on are padding; in each step some slot has exactly 384 live rows.
All inputs are finite; a program needn't handle non-finite values.
Results may differ from a plain program's by a relative error of at most 0.0074.
Values may be sent and summed in bfloat16 or wider, within the bound.
No kernel may reach another device: no remote copies, remote signals or barrier semaphores. Data moves between devices by JAX's collectives and lax.ppermute only.
A program may use at most 128 MiB of HBM per device.

v0:
```python
import jax
import jax.numpy as jnp
from jax import lax
from jax.sharding import PartitionSpec as P

D = 2048
FF = 512


beta_one = 0.9
beta_two = 0.99
rho_scale = 2.0
learn_rate = 0.005
grad_scale = 0.25


def silu_parts(values):
    sigmoid = jax.nn.sigmoid(values)
    return (values * sigmoid, sigmoid * (1.0 + values * (1.0 - sigmoid)))


def slot_backward(rows_one, cotangent, live_count, flat_weights):
    split_at = 2 * D * FF
    w_gateup = flat_weights[:split_at].reshape(D, 2 * FF)
    w_down = flat_weights[split_at:].reshape(FF, D)
    live = (jnp.arange(rows_one.shape[0], dtype=jnp.int32) < live_count)[:, None]
    masked_ct = jnp.where(live, cotangent, jnp.zeros_like(cotangent))
    preact = jnp.dot(rows_one, w_gateup, preferred_element_type=jnp.float32)
    gate_pre = preact[:, :FF]
    up_pre = preact[:, FF:]
    activated, slope = silu_parts(gate_pre)
    hidden = (activated * up_pre).astype(jnp.bfloat16)
    hidden_grad = lax.dot_general(
        masked_ct, w_down, (((1,), (1,)), ((), ())), preferred_element_type=jnp.float32
    )
    pre_grad = jnp.concatenate(
        [hidden_grad * up_pre * slope, hidden_grad * activated], axis=1
    ).astype(jnp.bfloat16)
    row_grad = lax.dot_general(
        pre_grad, w_gateup, (((1,), (1,)), ((), ())), preferred_element_type=jnp.float32
    ).astype(jnp.bfloat16)
    grad_gateup = lax.dot_general(
        rows_one, pre_grad, (((0,), (0,)), ((), ())), preferred_element_type=jnp.float32
    )
    grad_down = lax.dot_general(
        hidden, masked_ct, (((0,), (0,)), ((), ())), preferred_element_type=jnp.float32
    )
    return (row_grad, jnp.concatenate([grad_gateup.reshape(-1), grad_down.reshape(-1)]))


def sophia(grads, momentum, curvature, master):
    momentum = beta_one * momentum + (1.0 - beta_one) * grads
    curvature = beta_two * curvature + (1.0 - beta_two) * grads * grads
    master = master - learn_rate * jnp.clip(momentum / (rho_scale * curvature), -1.0, 1.0)
    return (momentum, curvature, master)


def body(token_rows, cotangents, row_counts, old_place, new_place, momentum, curvature, master):
    group_count = lax.axis_size("grp")
    slot_count = lax.axis_size("slot")
    device_count = group_count * slot_count
    experts = master.shape[0]
    per_group = experts // group_count
    shard_len = master.shape[1]
    owners = (jnp.arange(group_count, dtype=jnp.int32) * per_group)[None, :]
    outputs = []
    for step_index, place_map in ((0, old_place), (1, new_place)):
        weights_bf = master.astype(jnp.bfloat16)
        send_expert_ids = (place_map + owners).reshape(-1)
        outgoing = jnp.take(weights_bf, send_expert_ids, axis=0)
        send_arrived = lax.all_to_all(
            outgoing, ("slot", "grp"), split_axis=0, concat_axis=0, tiled=True
        )
        slot_weights = send_arrived.reshape(-1)
        row_grad, flat_grad = slot_backward(
            token_rows[step_index, 0, 0],
            cotangents[step_index, 0, 0],
            row_counts[step_index, 0, 0],
            slot_weights,
        )
        arrived = lax.all_to_all(
            flat_grad.reshape(device_count, shard_len),
            ("slot", "grp"),
            split_axis=0,
            concat_axis=0,
            tiled=True,
        )
        expert_ids = (place_map + owners).reshape(-1)
        selector = (expert_ids[None, :] == jnp.arange(experts, dtype=jnp.int32)[:, None]).astype(
            jnp.float32
        )
        totals = jnp.dot(
            selector, arrived, precision=lax.Precision.HIGHEST, preferred_element_type=jnp.float32
        )
        grads = totals * grad_scale
        momentum, curvature, master = sophia(grads, momentum, curvature, master)
        outputs.append(row_grad)
    return (jnp.stack(outputs)[:, None, None], momentum, curvature, master)


def solution(mesh):
    return jax.shard_map(
        body,
        mesh=mesh,
        in_specs=(
            P(None, "slot", "grp", None, None),
            P(None, "slot", "grp", None, None),
            P(None, "slot", "grp"),
            P(),
            P(),
            P(None, ("slot", "grp")),
            P(None, ("slot", "grp")),
            P(None, ("slot", "grp")),
        ),
        out_specs=(
            P(None, "slot", "grp", None, None),
            P(None, ("slot", "grp")),
            P(None, ("slot", "grp")),
            P(None, ("slot", "grp")),
        ),
        check_vma=False,
    )
```

profile of v0, /device:TPU:0, one launch (start us, length us, event | category | flops | bytes accessed | tf_op | source)
XLA Modules:
  0.0 863.2 jit_solution(14477004691764230249)
XLA Ops:
  17.0 9.0 %reduce.4 = bf16[128,24576]{1,0:T(8,128)(2,1)} reduce(bf16[128,1,24576]{2,0,1:T(8,128)(2,1)} %select_bitcast_fusion.1, bf16[]{:T(256)} %broadcast.120), dimensions={1}, to_apply=%copy.34.reduce_sub_computation | reduce | bytes 12582914 | tf_op jit(solution)/shard_map/all_to_all | solution.py:71
  26.0 9.4 %reshape.105 = bf16[128,2,12288]{2,1,0:T(2,128)(2,1)} reshape(bf16[128,24576]{1,0:T(8,128)(2,1)} %reduce.4) | data formatting | bytes 12582912
  35.4 12.1 %all-to-all-start = ((bf16[128,2,12288]{2,1,0:T(2,128)(2,1)}), bf16[128,2,12288]{2,1,0:T(2,128)(2,1)}, u32[]{:S(2)}, u32[]{:S(2)}) async-start(bf16[128,2,12288]{2,1,0:T(2,128)(2,1)} %reshape.105), calls=%async_computation | async-start | bytes 12582912 | tf_op jit(solution)/shard_map/all_to_all | solution.py:71
  48.7 74.7 %all-to-all-done = bf16[128,2,12288]{2,1,0:T(2,128)(2,1)} async-done(((bf16[128,2,12288]{2,1,0:T(2,128)(2,1)}), bf16[128,2,12288]{2,1,0:T(2,128)(2,1)}, u32[]{:S(2)}, u32[]{:S(2)}) %all-to-all-start) | async-done | bytes 6291488 | tf_op jit(solution)/shard_map/all_to_all | solution.py:71
  123.5 33.8 %reshape.106 = bf16[128,1,24576]{2,1,0:T(2,128)(2,1)} reshape(bf16[128,2,12288]{2,1,0:T(2,128)(2,1)} %all-to-all-done) | data formatting | bytes 12582912
  157.3 38.3 %reduce = bf16[128,24576]{1,0:T(8,128)(2,1)} reduce(bf16[128,1,24576]{2,1,0:T(2,128)(2,1)} %reshape.106, bf16[]{:T(256)} %constant.40), dimensions={1}, to_apply=%all_to_all.29.reduce_sub_computation | reduce | bytes 12582914 | tf_op jit(solution)/shard_map/all_to_all | solution.py:71
  195.6 8.8 %slice.58 = bf16[3072,1024]{1,0:T(8,128)(2,1)} reshape(bf16[128,24576]{1,0:T(8,128)(2,1)} %reduce) | data formatting | bytes 12582912 | tf_op jit(solution)/shard_map/slice | solution.py:24
  204.4 12.7 %slice.56 = bf16[1536,2048]{1,0:T(8,128)(2,1)} reshape(bf16[128,24576]{1,0:T(8,128)(2,1)} %reduce) | data formatting | bytes 12582912 | tf_op jit(solution)/shard_map/slice | solution.py:25
  234.1 9.2 %copy.37 = f32[2048,1024]{1,0:T(8,128)} copy(f32[2048,1024]{0,1:T(8,128)} %convolution_bitcast_fusion.1) | data formatting | bytes 16777216 | tf_op jit(solution)/shard_map/dot_general | solution.py:42
  249.0 9.3 %pad_maximum_fusion = f32[3145728]{0:T(1024)} fusion(f32[1048576]{0:T(1024)S(1)} %bitcast.76, f32[2097152]{0:T(1024)S(1)} %bitcast.72), kind=kLoop, calls=%fused_computation.2 | loop fusion | flops 3145728 | bytes 25165824 | tf_op jit(solution)/shard_map/concatenate | solution.py:48
  264.8 151.5 %all-to-all-done.1 = f32[128,1,24576]{2,1,0:T(1,128)} async-done(((f32[128,1,24576]{2,1,0:T(1,128)}), f32[128,1,24576]{2,1,0:T(1,128)}, u32[]{:S(2)}, u32[]{:S(2)}) %all-to-all-start.1) | async-done | bytes 12582944 | tf_op jit(solution)/shard_map/all_to_all | solution.py:81
  416.3 17.7 %fusion.64 = (bf16[16,24576]{1,0:T(8,128)(2,1)S(1)}, f32[16,24576]{1,0:T(8,128)}, f32[16,24576]{1,0:T(8,128)}) fusion(f32[16,24576]{1,0:T(8,128)} %param.17, f32[16,24576]{1,0:T(8,128)S(1)} %copy-done.2, f32[16,24576]{1,0:T(8,128)} %param.15, f32[128,1,24576]{2,1,0:T(1,128)} %all-to-all-done.1, s32[128]{0:T(128)S(1)} %reshape.73), kind=kOutput, calls=%fused_computation.88 | convolution fusion | flops 609486848 | bytes 21234176 | tf_op jit(solution)/shard_map/dot_general | solution.py:92
  447.3 9.0 %reduce.5 = bf16[128,24576]{1,0:T(8,128)(2,1)} reduce(bf16[128,1,24576]{2,0,1:T(8,128)(2,1)} %select_bitcast_fusion, bf16[]{:T(256)} %broadcast.120), dimensions={1}, to_apply=%copy.38.reduce_sub_computation | reduce | bytes 12582914 | tf_op jit(solution)/shard_map/all_to_all | solution.py:71
  456.3 9.4 %reshape.107 = bf16[128,2,12288]{2,1,0:T(2,128)(2,1)} reshape(bf16[128,24576]{1,0:T(8,128)(2,1)} %reduce.5) | data formatting | bytes 12582912
  465.7 9.8 %all-to-all-start.2 = ((bf16[128,2,12288]{2,1,0:T(2,128)(2,1)}), bf16[128,2,12288]{2,1,0:T(2,128)(2,1)}, u32[]{:S(2)}, u32[]{:S(2)}) async-start(bf16[128,2,12288]{2,1,0:T(2,128)(2,1)} %reshape.107), calls=%async_computation.2 | async-start | bytes 12582912 | tf_op jit(solution)/shard_map/all_to_all | solution.py:71
  476.2 75.3 %all-to-all-done.2 = bf16[128,2,12288]{2,1,0:T(2,128)(2,1)} async-done(((bf16[128,2,12288]{2,1,0:T(2,128)(2,1)}), bf16[128,2,12288]{2,1,0:T(2,128)(2,1)}, u32[]{:S(2)}, u32[]{:S(2)}) %all-to-all-start.2) | async-done | bytes 6291488 | tf_op jit(solution)/shard_map/all_to_all | solution.py:71
  551.5 33.8 %reshape.108 = bf16[128,1,24576]{2,1,0:T(2,128)(2,1)} reshape(bf16[128,2,12288]{2,1,0:T(2,128)(2,1)} %all-to-all-done.2) | data formatting | bytes 12582912
  585.3 38.3 %reduce.2 = bf16[128,24576]{1,0:T(8,128)(2,1)} reduce(bf16[128,1,24576]{2,1,0:T(2,128)(2,1)} %reshape.108, bf16[]{:T(256)} %constant.40), dimensions={1}, to_apply=%all_to_all.34.reduce_sub_computation | reduce | bytes 12582914 | tf_op jit(solution)/shard_map/all_to_all | solution.py:71
  623.6 9.0 %slice.67 = bf16[3072,1024]{1,0:T(8,128)(2,1)} reshape(bf16[128,24576]{1,0:T(8,128)(2,1)} %reduce.2) | data formatting | bytes 12582912 | tf_op jit(solution)/shard_map/slice | solution.py:24
  632.6 12.6 %slice.65 = bf16[1536,2048]{1,0:T(8,128)(2,1)} reshape(bf16[128,24576]{1,0:T(8,128)(2,1)} %reduce.2) | data formatting | bytes 12582912 | tf_op jit(solution)/shard_map/slice | solution.py:25
  662.6 9.2 %copy.40 = f32[2048,1024]{1,0:T(8,128)} copy(f32[2048,1024]{0,1:T(8,128)} %convolution_bitcast_fusion) | data formatting | bytes 16777216 | tf_op jit(solution)/shard_map/dot_general | solution.py:42
  677.5 9.3 %pad_maximum_fusion.1 = f32[3145728]{0:T(1024)} fusion(f32[1048576]{0:T(1024)S(1)} %bitcast.77, f32[2097152]{0:T(1024)S(1)} %bitcast.73), kind=kLoop, calls=%fused_computation.3 | loop fusion | flops 3145728 | bytes 25165824 | tf_op jit(solution)/shard_map/concatenate | solution.py:48
  703.1 141.8 %all-to-all-done.3 = f32[128,1,24576]{2,1,0:T(1,128)} async-done(((f32[128,1,24576]{2,1,0:T(1,128)}), f32[128,1,24576]{2,1,0:T(1,128)}, u32[]{:S(2)}, u32[]{:S(2)}) %all-to-all-start.3) | async-done | bytes 12582944 | tf_op jit(solution)/shard_map/all_to_all | solution.py:81
  844.8 18.2 %multiply_subtract_fusion = (f32[16,24576]{1,0:T(8,128)}, f32[16,24576]{1,0:T(8,128)}, f32[16,24576]{1,0:T(8,128)}) fusion(f32[16,24576]{1,0:T(8,128)} %get-tuple-element.25, f32[16,24576]{1,0:T(8,128)} %get-tuple-element.34, f32[16,24576]{1,0:T(8,128)S(1)} %copy-done.2, f32[16,24576]{1,0:T(8,128)} %param.15, f32[128,1,24576]{2,1,0:T(1,128)} %all-to-all-done.3, ...), kind=kOutput, calls=%fused_computation.39 | convolution fusion | flops 612239360 | bytes 23593472 | tf_op jit(solution)/shard_map/dot_general | solution.py:92
  (58 shorter events, 99.8 us)
Async XLA Ops:
  35.4 12.1 %copy-start.7 = (s32[2,1,1]{0,2,1:T(1,128)S(1)}, s32[2,1,1]{0,2,1:T(1,128)}, u32[]{:S(2)}) copy-start(s32[2,1,1]{0,2,1:T(1,128)} %param.12) | copy-start | bytes 28
  35.4 88.1 %all-to-all-start = ((bf16[128,2,12288]{2,1,0:T(2,128)(2,1)}), bf16[128,2,12288]{2,1,0:T(2,128)(2,1)}, u32[]{:S(2)}, u32[]{:S(2)}) async-start(bf16[128,2,12288]{2,1,0:T(2,128)(2,1)} %reshape.105), calls=%async_computation | async-start | bytes 12582912 | tf_op jit(solution)/shard_map/all_to_all | solution.py:71
  204.4 12.7 %copy-start.3 = (bf16[2,1,1,384,2048]{4,3,2,1,0:T(8,128)(2,1)S(1)}, bf16[2,1,1,384,2048]{4,3,2,1,0:T(8,128)(2,1)}, u32[]{:S(2)}) copy-start(bf16[2,1,1,384,2048]{4,3,2,1,0:T(8,128)(2,1)} %param.10) | copy-start | bytes 9437188
  217.2 4.1 copy-start.8
  225.6 2.9 copy-start.5
  243.3 5.7 copy-start
  258.3 158.0 %copy-start.2 = (f32[16,24576]{1,0:T(8,128)S(1)}, f32[16,24576]{1,0:T(8,128)}, u32[]{:S(2)}) copy-start(f32[16,24576]{1,0:T(8,128)} %param.16) | copy-start | bytes 4718596
  258.3 158.0 %all-to-all-start.1 = ((f32[128,1,24576]{2,1,0:T(1,128)}), f32[128,1,24576]{2,1,0:T(1,128)}, u32[]{:S(2)}, u32[]{:S(2)}) async-start(f32[128,1,24576]{2,1,0:T(1,128)} %bitcast.71), calls=%async_computation.1 | async-start | bytes 25165824 | tf_op jit(solution)/shard_map/all_to_all | solution.py:81
  465.7 85.8 %all-to-all-start.2 = ((bf16[128,2,12288]{2,1,0:T(2,128)(2,1)}), bf16[128,2,12288]{2,1,0:T(2,128)(2,1)}, u32[]{:S(2)}, u32[]{:S(2)}) async-start(bf16[128,2,12288]{2,1,0:T(2,128)(2,1)} %reshape.107), calls=%async_computation.2 | async-start | bytes 12582912 | tf_op jit(solution)/shard_map/all_to_all | solution.py:71
  645.2 4.6 copy-start.9
  654.1 2.9 copy-start.4
  671.9 5.7 copy-start.1
  686.8 6.3 copy-start.6
  686.8 158.0 %all-to-all-start.3 = ((f32[128,1,24576]{2,1,0:T(1,128)}), f32[128,1,24576]{2,1,0:T(1,128)}, u32[]{:S(2)}, u32[]{:S(2)}) async-start(f32[128,1,24576]{2,1,0:T(1,128)} %bitcast.70), calls=%async_computation.3 | async-start | bytes 25165824 | tf_op jit(solution)/shard_map/all_to_all | solution.py:81
where the time goes:
time: 876 us; the launch traced here: 863 us
  waiting for transfers between devices  443 us (51%)
  local copies, waits for them, and re-layouts  181 us (21%)
  other arithmetic  131 us (15%)
  matrix products  72.4 us (8%)
  starting transfers between devices  34.5 us (4%)
    all_to_all x2, waiting for transfers between devices, body(): lax.all_to_all(flat_grad.reshape(device_count, shard_len), ('slot', 'grp'...  293 us
    all_to_all x2, waiting for transfers between devices, body(): lax.all_to_all(outgoing, ('slot', 'grp'), split_axis=0, concat_axis=0, ti...  150 us
    all_to_all x6, other arithmetic, body(): lax.all_to_all(outgoing, ('slot', 'grp'), split_axis=0, concat_axis=0, ti...  107 us
    unnamed x28, local copies, waits for them, and re-layouts  103 us
    dot_general x2, matrix products, body(): jnp.dot(selector, arrived, precision=lax.Precision.HIGHEST, preferred_ele...  35.9 us
    slice x2, local copies, waits for them, and re-layouts, slot_backward(): w_down = flat_weights[split_at:].reshape(FF, D)  25.3 us
    all_to_all x2, starting transfers between devices, body(): lax.all_to_all(outgoing, ('slot', 'grp'), split_axis=0, concat_axis=0, ti...  21.9 us
    concatenate x2, other arithmetic, slot_backward(): jnp.concatenate([grad_gateup.reshape(-1), grad_down.reshape(-1)])  18.6 us
  transfers between devices with their start and end apart: 4, of which 4 were waited for; matrix products, arithmetic and copies ran while one was open for 1% of the time, Pallas kernels for 0%

commit v1 on v0

v1 whole, which is shorter than its diff:
```python
import jax
import jax.numpy as jnp
from jax import lax
from jax.experimental import pallas as pl
from jax.experimental.pallas import tpu as pltpu
from jax.sharding import PartitionSpec as P

D = 2048
FF = 512
ROWS = 384
WIDE = 1024
BLK = 96
NBLK = 32
PIECE = 24
SPLIT = 21
HEAD = 32

beta_one = 0.9
beta_two = 0.99
rho_scale = 2.0
learn_rate = 0.005
grad_scale = 0.25

F32 = jnp.float32
BF16 = jnp.bfloat16
VMEM = pltpu.VMEM
SMEM = pltpu.SMEM


def params(limit_mb, **more):
    return pltpu.CompilerParams(vmem_limit_bytes=limit_mb * 1024 * 1024, **more)


def wire_row(block, local):
    base = jnp.where(block == SPLIT, HEAD, 0)
    half = jnp.where(block == SPLIT, (BLK - HEAD) // 2, BLK // 2)
    inner = local - base
    moved = base + lax.rem(inner, 2) * half + lax.div(inner, 2)
    is_down = (block > SPLIT) | ((block == SPLIT) & (local >= HEAD))
    return jnp.where(is_down, moved, local)


def pack_kernel(where_ref, place_ref, p0, p1, p2, p3, out_ref, f32_ref, rows_ref, bf_ref, sem):
    block = where_ref[0]
    group = where_ref[1]
    for shift, piece in enumerate((p0, p1, p2, p3)):
        f32_ref[...] = piece[...].astype(F32)
        source = lax.rem(group - shift + 4, 4)

        for j in range(PIECE):
            row = wire_row(block, PIECE * source + j)
            for e in range(4):
                rows_ref[e, pl.ds(row, 1), :] = f32_ref[e : e + 1, j * WIDE : (j + 1) * WIDE]
    bf_ref[...] = rows_ref[...].astype(BF16)

    @pl.loop(0, NBLK)
    def _(s):
        pltpu.make_async_copy(bf_ref.at[place_ref[s]], out_ref.at[s], sem).start()

    pltpu.make_async_copy(out_ref, out_ref, sem).wait()


def pack(where, place, pieces):
    return pl.pallas_call(
        pack_kernel,
        out_shape=jax.ShapeDtypeStruct((NBLK, BLK, WIDE), BF16),
        in_specs=[pl.BlockSpec(memory_space=SMEM)] * 2 + [pl.BlockSpec(memory_space=VMEM)] * 4,
        out_specs=pl.BlockSpec(memory_space=pl.ANY),
        scratch_shapes=[
            VMEM((4, PIECE * WIDE), F32),
            VMEM((4, BLK, WIDE), F32),
            VMEM((4, BLK, WIDE), BF16),
            pltpu.SemaphoreType.DMA,
        ],
        compiler_params=params(32),
        name="pack",
    )(where, place, *pieces)


def down_spans():
    first = SPLIT * BLK + HEAD
    count = (BLK - HEAD) // 2
    spans = [(0, count, first, first + count)]
    done = count
    for block in range(SPLIT + 1, NBLK):
        spans.append((done, BLK // 2, block * BLK, block * BLK + BLK // 2))
        done += BLK // 2
    return spans


NT = (((1,), (1,)), ((), ()))
NN = (((1,), (0,)), ((), ()))


def dot(a, b, dims):
    return lax.dot_general(a, b, dims, preferred_element_type=F32)


def expert_kernel(count_ref, x_ref, xt_ref, dy_ref, w_ref, g_ref, dz_ref, dym_ref, wd_ref, h_ref, ht_ref):
    live = lax.broadcasted_iota(jnp.int32, (ROWS, 1), 0) < count_ref[0]
    dym_ref[...] = jnp.where(live, dy_ref[...], jnp.zeros((), BF16))
    for first, count, left, right in down_spans():
        wd_ref[first : first + count, :WIDE] = w_ref[left : left + count, :]
        wd_ref[first : first + count, WIDE:] = w_ref[right : right + count, :]
    tile = 256
    for n in range(FF // tile):
        cols = slice(n * tile, (n + 1) * tile)
        ups = slice(FF + n * tile, FF + (n + 1) * tile)
        gate = dot(x_ref[...], w_ref[:D, cols], NN)
        up = dot(x_ref[...], w_ref[:D, ups], NN)
        dh = dot(dym_ref[...], wd_ref[cols, :], NT)
        sig = jax.nn.sigmoid(gate)
        act = gate * sig
        slope = sig * (1.0 + gate * (1.0 - sig))
        h_ref[:, cols] = (act * up).astype(BF16)
        dz_ref[:, cols] = (dh * up * slope).astype(BF16)
        dz_ref[:, ups] = (dh * act).astype(BF16)
    ht_ref[...] = h_ref[...].T

    @pl.loop(0, D // tile)
    def _(i):
        rows = pl.ds(pl.multiple_of(i * tile, tile), tile)
        g_ref[rows, :] = dot(xt_ref[rows, :], dz_ref[...], NN).astype(BF16)

    for first, count, left, right in down_spans():
        part = dot(ht_ref[first : first + count, :], dym_ref[...], NN).astype(BF16)
        g_ref[left : left + count, :] = part[:, :WIDE]
        g_ref[right : right + count, :] = part[:, WIDE:]


def expert(count, x, xt, dy, weights):
    return pl.pallas_call(
        expert_kernel,
        out_shape=(
            jax.ShapeDtypeStruct((NBLK * BLK, WIDE), BF16),
            jax.ShapeDtypeStruct((ROWS, 2 * FF), BF16),
        ),
        in_specs=[pl.BlockSpec(memory_space=SMEM)] + [pl.BlockSpec(memory_space=VMEM)] * 4,
        out_specs=(pl.BlockSpec(memory_space=VMEM), pl.BlockSpec(memory_space=VMEM)),
        scratch_shapes=[
            VMEM((ROWS, D), BF16),
            VMEM((FF, D), BF16),
            VMEM((ROWS, FF), BF16),
            VMEM((FF, ROWS), BF16),
        ],
        compiler_params=params(48),
        name="expert",
    )(count, x, xt, dy, weights)


def row_grad_kernel(dz_ref, w_ref, out_ref):
    out_ref[...] = dot(dz_ref[...], w_ref[...], NT).astype(BF16)


def row_grad(dz, weights):
    tile = 256
    return pl.pallas_call(
        row_grad_kernel,
        grid=(D // tile,),
        out_shape=jax.ShapeDtypeStruct((ROWS, D), BF16),
        in_specs=[
            pl.BlockSpec((ROWS, 2 * FF), lambda i: (0, 0)),
            pl.BlockSpec((tile, WIDE), lambda i: (i, 0)),
        ],
        out_specs=pl.BlockSpec((ROWS, tile), lambda i: (0, i)),
        compiler_params=params(32),
        cost_estimate=pl.CostEstimate(flops=2 * ROWS * D * 2 * FF, bytes_accessed=8 << 20, transcendentals=0),
        name="row_grad",
    )(dz, weights)


def reduce_kernel(where_ref, place_ref, in_ref, o0, o1, o2, o3, acc_ref, line_ref):
    step = pl.program_id(0)

    @pl.when(step == 0)
    def _():
        acc_ref[...] = jnp.zeros_like(acc_ref)

    for k in range(4):
        e = place_ref[4 * step + k]
        acc_ref[e] += in_ref[k].astype(F32)

    @pl.when(step == pl.num_programs(0) - 1)
    def _():
        block = where_ref[0]
        group = where_ref[1]
        for shift, out in enumerate((o0, o1, o2, o3)):
            target = lax.rem(group + shift, 4)
            for j in range(PIECE):
                row = wire_row(block, PIECE * target + j)
                for e in range(4):
                    line_ref[e : e + 1, j * WIDE : (j + 1) * WIDE] = acc_ref[e, pl.ds(row, 1), :]
            out[...] = line_ref[...].astype(BF16)


def reduce(where, place, arrived):
    piece = jax.ShapeDtypeStruct((4, PIECE * WIDE), BF16)
    whole = pl.BlockSpec((4, PIECE * WIDE), lambda i: (0, 0))
    return pl.pallas_call(
        reduce_kernel,
        grid=(NBLK // 4,),
        out_shape=(piece,) * 4,
        in_specs=[pl.BlockSpec(memory_space=SMEM)] * 2 + [pl.BlockSpec((4, BLK, WIDE), lambda i: (i, 0, 0))],
        out_specs=(whole,) * 4,
        scratch_shapes=[VMEM((4, BLK, WIDE), F32), VMEM((4, PIECE * WIDE), F32)],
        compiler_params=params(32),
        name="reduce",
    )(where, place, arrived)


def sophia_kernel(where_ref, p0, p1, p2, p3, m_ref, c_ref, w_ref, mo_ref, co_ref, wo_ref, g_ref):
    group = where_ref[1]
    for shift, piece in enumerate((p0, p1, p2, p3)):
        source = lax.rem(group - shift + 4, 4)
        values = piece[...].astype(F32)
        for e in range(4):
            g_ref[pl.ds(4 * source + e, 1), :] = values[e : e + 1, :]
    grads = g_ref[...] * grad_scale
    momentum = beta_one * m_ref[...] + (1.0 - beta_one) * grads
    curvature = beta_two * c_ref[...] + (1.0 - beta_two) * grads * grads
    mo_ref[...] = momentum
    co_ref[...] = curvature
    wo_ref[...] = w_ref[...] - learn_rate * jnp.clip(momentum / (rho_scale * curvature), -1.0, 1.0)


def sophia(where, pieces, momentum, curvature, master):
    experts, length = master.shape
    tile = 4096
    state = pl.BlockSpec((experts, tile), lambda i: (0, i))
    return pl.pallas_call(
        sophia_kernel,
        grid=(length // tile,),
        out_shape=(jax.ShapeDtypeStruct(master.shape, F32),) * 3,
        in_specs=[pl.BlockSpec(memory_space=SMEM)] + [pl.BlockSpec((4, tile), lambda i: (0, i))] * 4 + [state] * 3,
        out_specs=(state,) * 3,
        scratch_shapes=[VMEM((experts, tile), F32)],
        compiler_params=params(32),
        name="sophia",
    )(where, *pieces, momentum, curvature, master)


def swap_y(pieces):
    out = [pieces[0]]
    for shift in (1, 2, 3):
        out.append(lax.ppermute(pieces[shift], "grp", [(g, (g + shift) % 4) for g in range(4)]))
    return out


def body(token_rows, cotangents, row_counts, old_place, new_place, momentum, curvature, master):
    group = lax.axis_index("grp")
    block = lax.axis_index("slot")
    where = jnp.stack([block, group]).astype(jnp.int32)
    outputs = []
    for step, place_map in ((0, old_place), (1, new_place)):
        place = lax.dynamic_index_in_dim(place_map, group, 1, keepdims=False)
        x, dy = token_rows[step, 0, 0], cotangents[step, 0, 0]
        count = row_counts[step].reshape(1)
        sends = [
            lax.dynamic_slice_in_dim(master, 4 * lax.rem(group + k, 4), 4, 0).astype(BF16)
            for k in range(4)
        ]
        outgoing = pack(where, place, swap_y(sends))
        weights = lax.all_to_all(outgoing, "slot", 0, 0, tiled=True).reshape(NBLK * BLK, WIDE)
        grads, dz = expert(count, x, x.T, dy, weights)
        arrived = lax.all_to_all(grads.reshape(NBLK, BLK, WIDE), "slot", 0, 0, tiled=True)
        outputs.append(row_grad(dz, weights))
        pieces = swap_y(reduce(where, place, arrived))
        momentum, curvature, master = sophia(where, pieces, momentum, curvature, master)
    return (jnp.stack(outputs)[:, None, None], momentum, curvature, master)


def solution(mesh):
    tokens = P(None, "slot", "grp", None, None)
    state = P(None, ("slot", "grp"))
    return jax.shard_map(
        body,
        mesh=mesh,
        in_specs=(tokens, tokens, P(None, "slot", "grp"), P(), P(), state, state, state),
        out_specs=(tokens, state, state, state),
        check_vma=False,
    )
```

time: 876 us -> 466 us (0.53); the launches traced: 863 us -> 465 us
  waiting for transfers between devices: 443 us -> 242 us
  local copies, waits for them, and re-layouts: 181 us -> 29.3 us
  other arithmetic: 131 us -> 2.01 us
  Pallas kernels: 0 us -> 79.6 us
  blocking collectives: 0 us -> 77.6 us
  matrix products: 72.4 us -> 0 us
    all_to_all x4 -> x3, waiting for transfers between devices: 443 us -> 207 us  [the longest x2 142 us: body(): lax.all_to_all(outgoing, 'slot', 0, 0, tiled=True).reshape(NBLK * BLK, WIDE)]
    all_to_all x6 -> x0, other arithmetic: 107 us -> none  [body(): lax.all_to_all(outgoing, ('slot', 'grp'), split_axis=0, concat_axis=0, ti...]
    unnamed x28 -> x44, local copies, waits for them, and re-layouts: 103 us -> 17.2 us
    pallas_call x0 -> x10, Pallas kernels: none -> 79.6 us  [the longest x2 31 us: expert(): pl.pallas_call(expert_kernel, out_shape=(jax.ShapeDtypeStruct((NBLK * BLK...]
    all_to_all x0 -> x1, blocking collectives: none -> 77.6 us  [body(): lax.all_to_all(grads.reshape(NBLK, BLK, WIDE), 'slot', 0, 0, tiled=True)]
    dot_general x12 -> x0, matrix products: 72.4 us -> none  [the longest x2 35.9 us: body(): jnp.dot(selector, arrived, precision=lax.Precision.HIGHEST, preferred_ele...]
    slice x5 -> x2, local copies, waits for them, and re-layouts: 43.8 us -> 4.87 us  [the longest x1 4.26 us: body(): x, dy = (token_rows[step, 0, 0], cotangents[step, 0, 0])]
    ppermute x0 -> x12, waiting for transfers between devices: none -> 34.8 us  [swap_y(): lax.ppermute(pieces[shift], 'grp', [(g, (g + shift) % 4) for g in range(4)])]
  transfers between devices with their start and end apart: 4 -> 15, of which waited for: 4 -> 13; matrix products, arithmetic and copies ran while one was open for 1% -> 3% of each run, Pallas kernels for 0% -> 3%
where the time goes in v1:
time: 466 us; the launch traced here: 465 us
  waiting for transfers between devices  242 us (52%)
  Pallas kernels  79.6 us (17%)
  blocking collectives  77.6 us (17%)
  starting transfers between devices  33.2 us (7%)
  local copies, waits for them, and re-layouts  29.3 us (6%)
    all_to_all x2, waiting for transfers between devices, body(): lax.all_to_all(outgoing, 'slot', 0, 0, tiled=True).reshape(NBLK * BLK, WIDE)  142 us
    all_to_all x1, blocking collectives, body(): lax.all_to_all(grads.reshape(NBLK, BLK, WIDE), 'slot', 0, 0, tiled=True)  77.6 us
    all_to_all x1, waiting for transfers between devices, body(): lax.all_to_all(grads.reshape(NBLK, BLK, WIDE), 'slot', 0, 0, tiled=True)  64.9 us
    ppermute x12, waiting for transfers between devices, swap_y(): lax.ppermute(pieces[shift], 'grp', [(g, (g + shift) % 4) for g in range(4)])  34.8 us
    pallas_call x2, Pallas kernels, expert(): pl.pallas_call(expert_kernel, out_shape=(jax.ShapeDtypeStruct((NBLK * BLK...  31 us
    pallas_call x2, Pallas kernels, pack(): pl.pallas_call(pack_kernel, out_shape=jax.ShapeDtypeStruct((NBLK, BLK, WI...  19.4 us
    unnamed x44, local copies, waits for them, and re-layouts  17.2 us
    ppermute x12, starting transfers between devices, swap_y(): lax.ppermute(pieces[shift], 'grp', [(g, (g + shift) % 4) for g in range(4)])  14.9 us
  transfers between devices with their start and end apart: 15, of which 13 were waited for; matrix products, arithmetic and copies ran while one was open for 3% of the time, Pallas kernels for 3%

profile of v1, /device:TPU:0, one launch (start us, length us, event | category | flops | bytes accessed | tf_op | source)
XLA Modules:
  0.0 464.7 jit_solution(7001356228668007656)
XLA Ops:
  3.0 3.1 collective-permute-start.2
  7.8 6.6 %collective-permute-done.2.p3 = bf16[4,24576]{1,0:T(4,128)(2,1)S(1)} collective-permute-done((bf16[4,24576]{1,0:T(4,128)(2,1)S(1)}, bf16[4,24576]{1,0:T(4,128)(2,1)S(1)}, u32[]{:S(2)}, u32[]{:S(2)}) %collective-permute-start.2) | collective-permute-done | bytes 196640 | tf_op jit(solution)/shard_map/ppermute | solution.py:245
  18.2 9.7 %pack.2 = bf16[32,96,1024]{2,1,0:T(8,128)(2,1)S(1)} custom-call(s32[2]{0:T(128)S(1)} %pad_add_fusion.where_ref, s32[32]{0:T(128)S(1)} %fusion.place_ref, bf16[4,24576]{1,0:T(4,128)(2,1)S(1)} %get-tuple-element.57.p0, bf16[4,24576]{1,0:T(4,128)(2,1)S(1)} %collective-permute-done.p1, bf16[4,24576]{1,0:T(4,128)(2,1)S(1)} %collective-permute-done.1.p2, ...), custom_call_target="tpu_custom_call" | custom-call | tf_op jit(solution)/shard_map/pack/pallas_call | solution.py:64
  30.5 8.3 %all-to-all-start = ((bf16[32,96,1024]{2,1,0:T(8,128)(2,1)}), bf16[32,96,1024]{2,1,0:T(8,128)(2,1)}, u32[]{:S(2)}, u32[]{:S(2)}) async-start(bf16[32,96,1024]{2,1,0:T(8,128)(2,1)} %copy-done.2), calls=%async_computation | async-start | bytes 12582912 | tf_op jit(solution)/shard_map/all_to_all | solution.py:263
  38.8 4.3 fusion.2
  46.3 4.0 slice_bitcast_fusion.1
  50.2 66.5 %all-to-all-done = bf16[32,96,1024]{2,1,0:T(8,128)(2,1)} async-done(((bf16[32,96,1024]{2,1,0:T(8,128)(2,1)}), bf16[32,96,1024]{2,1,0:T(8,128)(2,1)}, u32[]{:S(2)}, u32[]{:S(2)}) %all-to-all-start) | async-done | bytes 6291488 | tf_op jit(solution)/shard_map/all_to_all | solution.py:263
  119.5 15.6 %expert.2 = (bf16[3072,1024]{1,0:T(8,128)(2,1)}, bf16[384,1024]{1,0:T(8,128)(2,1)S(1)}) custom-call(s32[1]{0:T(128)} %bitcast.count_ref, bf16[384,2048]{1,0:T(8,128)(2,1)S(1)} %get-tuple-element.47.x_ref, bf16[2048,384]{1,0:T(8,128)(2,1)S(1)} %bitcast.32, bf16[384,2048]{1,0:T(8,128)(2,1)S(1)} %copy-done.6, bf16[3072,1024]{1,0:T(8,128)(2,1)} %bitcast.7.w_ref), custom_call_target="tpu_custom_call" | custom-call | tf_op jit(solution)/shard_map/expert/pallas_call | solution.py:132
  135.1 77.6 %all_to_all.20.in_ref = bf16[32,96,1024]{2,1,0:T(8,128)(2,1)S(1)} all-to-all(bf16[32,96,1024]{2,1,0:T(8,128)(2,1)} %bitcast.37), channel_id=1, replica_groups=mesh['slot'=32,'grp'=4] {'slot'}, dimensions={0} | all-to-all | bytes 12582912 | tf_op jit(solution)/shard_map/all_to_all | solution.py:265
  212.7 2.8 reduce.2
  218.8 9.1 %collective-permute-done.3.p1 = bf16[4,24576]{1,0:T(4,128)(2,1)S(1)} collective-permute-done((bf16[4,24576]{1,0:T(4,128)(2,1)S(1)}, bf16[4,24576]{1,0:T(4,128)(2,1)S(1)}, u32[]{:S(2)}, u32[]{:S(2)}) %collective-permute-start.3) | collective-permute-done | bytes 196640 | tf_op jit(solution)/shard_map/ppermute | solution.py:245
  228.5 2.9 sophia.2
  238.3 6.6 %collective-permute-done.8.p3 = bf16[4,24576]{1,0:T(4,128)(2,1)S(1)} collective-permute-done((bf16[4,24576]{1,0:T(4,128)(2,1)S(1)}, bf16[4,24576]{1,0:T(4,128)(2,1)S(1)}, u32[]{:S(2)}, u32[]{:S(2)}) %collective-permute-start.8) | collective-permute-done | bytes 196640 | tf_op jit(solution)/shard_map/ppermute | solution.py:245
  248.3 9.7 %pack.3 = bf16[32,96,1024]{2,1,0:T(8,128)(2,1)S(1)} custom-call(s32[2]{0:T(128)S(1)} %pad_add_fusion.where_ref, s32[32]{0:T(128)S(1)} %fusion.1.place_ref, bf16[4,24576]{1,0:T(4,128)(2,1)S(1)} %get-tuple-element.53.p0, bf16[4,24576]{1,0:T(4,128)(2,1)S(1)} %collective-permute-done.6.p1, bf16[4,24576]{1,0:T(4,128)(2,1)S(1)} %collective-permute-done.7.p2, ...), custom_call_target="tpu_custom_call" | custom-call | tf_op jit(solution)/shard_map/pack/pallas_call | solution.py:64
  260.6 4.9 %all-to-all-start.2 = ((bf16[32,96,1024]{2,1,0:T(8,128)(2,1)}), bf16[32,96,1024]{2,1,0:T(8,128)(2,1)}, u32[]{:S(2)}, u32[]{:S(2)}) async-start(bf16[32,96,1024]{2,1,0:T(8,128)(2,1)} %copy-done.3), calls=%async_computation.2 | async-start | bytes 12582912 | tf_op jit(solution)/shard_map/all_to_all | solution.py:263
  267.4 76.0 %all-to-all-done.2 = bf16[32,96,1024]{2,1,0:T(8,128)(2,1)} async-done(((bf16[32,96,1024]{2,1,0:T(8,128)(2,1)}), bf16[32,96,1024]{2,1,0:T(8,128)(2,1)}, u32[]{:S(2)}, u32[]{:S(2)}) %all-to-all-start.2) | async-done | bytes 6291488 | tf_op jit(solution)/shard_map/all_to_all | solution.py:263
  344.8 15.5 %expert.3 = (bf16[3072,1024]{1,0:T(8,128)(2,1)}, bf16[384,1024]{1,0:T(8,128)(2,1)S(1)}) custom-call(s32[1]{0:T(128)} %bitcast.9.count_ref, bf16[384,2048]{1,0:T(8,128)(2,1)S(1)} %get-tuple-element.48.x_ref, bf16[2048,384]{1,0:T(8,128)(2,1)S(1)} %bitcast.33, bf16[384,2048]{1,0:T(8,128)(2,1)S(1)} %copy-done.5, bf16[3072,1024]{1,0:T(8,128)(2,1)} %bitcast.15.w_ref), custom_call_target="tpu_custom_call" | custom-call | tf_op jit(solution)/shard_map/expert/pallas_call | solution.py:132
  361.2 5.0 %all-to-all-start.3 = ((bf16[32,96,1024]{2,1,0:T(8,128)(2,1)}), bf16[32,96,1024]{2,1,0:T(8,128)(2,1)}, u32[]{:S(2)}, u32[]{:S(2)}) async-start(bf16[32,96,1024]{2,1,0:T(8,128)(2,1)} %bitcast.36), calls=%async_computation.3 | async-start | bytes 12582912 | tf_op jit(solution)/shard_map/all_to_all | solution.py:265
  366.2 6.5 %row_grad.2 = bf16[384,2048]{1,0:T(8,128)(2,1)S(1)} custom-call(bf16[384,1024]{1,0:T(8,128)(2,1)S(1)} %copy-done.17, bf16[3072,1024]{1,0:T(8,128)(2,1)} %bitcast.7.w_ref), custom_call_target="tpu_custom_call" | custom-call | flops 1610612736 | bytes 8388608 | tf_op jit(solution)/shard_map/row_grad/pallas_call | solution.py:157
  372.8 6.5 %row_grad.3 = bf16[384,2048]{1,0:T(8,128)(2,1)S(1)} custom-call(bf16[384,1024]{1,0:T(8,128)(2,1)S(1)} %copy-done.19, bf16[3072,1024]{1,0:T(8,128)(2,1)} %bitcast.15.w_ref), custom_call_target="tpu_custom_call" | custom-call | flops 1610612736 | bytes 8388608 | tf_op jit(solution)/shard_map/row_grad/pallas_call | solution.py:157
  379.3 64.9 %all-to-all-done.3.in_ref = bf16[32,96,1024]{2,1,0:T(8,128)(2,1)} async-done(((bf16[32,96,1024]{2,1,0:T(8,128)(2,1)}), bf16[32,96,1024]{2,1,0:T(8,128)(2,1)}, u32[]{:S(2)}, u32[]{:S(2)}) %all-to-all-start.3) | async-done | bytes 6291488 | tf_op jit(solution)/shard_map/all_to_all | solution.py:265
  444.1 6.4 %reduce.3 = (bf16[4,24576]{1,0:T(4,128)(2,1)S(1)}, bf16[4,24576]{1,0:T(4,128)(2,1)S(1)}, bf16[4,24576]{1,0:T(4,128)(2,1)S(1)}, bf16[4,24576]{1,0:T(4,128)(2,1)S(1)}) custom-call(s32[2]{0:T(128)S(1)} %pad_add_fusion.where_ref, s32[32]{0:T(128)S(1)} %fusion.1.place_ref, bf16[32,96,1024]{2,1,0:T(8,128)(2,1)} %all-to-all-done.3.in_ref), custom_call_target="tpu_custom_call" | custom-call | tf_op jit(solution)/shard_map/reduce/pallas_call | solution.py:199
  455.8 3.8 collective-permute-done.9.p1
  460.5 4.2 sophia.3
  (70 shorter events, 43.6 us)
Async XLA Ops:
  0.6 7.2 %copy-start = (s32[32,4]{0,1:T(4,128)S(1)}, s32[32,4]{0,1:T(4,128)}, u32[]{:S(2)}) copy-start(s32[32,4]{0,1:T(4,128)} %param.11) | copy-start | bytes 1540
  3.0 11.5 %collective-permute-start.2 = (bf16[4,24576]{1,0:T(4,128)(2,1)S(1)}, bf16[4,24576]{1,0:T(4,128)(2,1)S(1)}, u32[]{:S(2)}, u32[]{:S(2)}) collective-permute-start(bf16[4,24576]{1,0:T(4,128)(2,1)S(1)} %get-tuple-element.54), channel_id=1, source_target_pairs={{0,3},{1,0},{2,1},{3,2},{4,7},{5,4},{6,5},{7,6},{8,11},{9,8},{10,9... | collective-permute-start | bytes 589832 | tf_op jit(solution)/shard_map/ppermute | solution.py:245
  6.1 9.4 %collective-permute-start.1 = (bf16[4,24576]{1,0:T(4,128)(2,1)S(1)}, bf16[4,24576]{1,0:T(4,128)(2,1)S(1)}, u32[]{:S(2)}, u32[]{:S(2)}) collective-permute-start(bf16[4,24576]{1,0:T(4,128)(2,1)S(1)} %get-tuple-element.55), channel_id=1, source_target_pairs={{0,2},{1,3},{2,0},{3,1},{4,6},{5,7},{6,4},{7,5},{8,10},{9,11},{10,... | collective-permute-start | bytes 589832 | tf_op jit(solution)/shard_map/ppermute | solution.py:245
  6.7 11.4 %collective-permute-start = (bf16[4,24576]{1,0:T(4,128)(2,1)S(1)}, bf16[4,24576]{1,0:T(4,128)(2,1)S(1)}, u32[]{:S(2)}, u32[]{:S(2)}) collective-permute-start(bf16[4,24576]{1,0:T(4,128)(2,1)S(1)} %get-tuple-element.56), channel_id=1, source_target_pairs={{0,1},{1,2},{2,3},{3,0},{4,5},{5,6},{6,7},{7,4},{8,9},{9,10},{10,1... | collective-permute-start | bytes 589832 | tf_op jit(solution)/shard_map/ppermute | solution.py:245
  30.5 86.2 %all-to-all-start = ((bf16[32,96,1024]{2,1,0:T(8,128)(2,1)}), bf16[32,96,1024]{2,1,0:T(8,128)(2,1)}, u32[]{:S(2)}, u32[]{:S(2)}) async-start(bf16[32,96,1024]{2,1,0:T(8,128)(2,1)} %copy-done.2), calls=%async_computation | async-start | bytes 12582912 | tf_op jit(solution)/shard_map/all_to_all | solution.py:263
  135.1 77.6 %copy-start.16 = (bf16[384,1024]{1,0:T(8,128)(2,1)}, bf16[384,1024]{1,0:T(8,128)(2,1)S(1)}, u32[]{:S(2)}) copy-start(bf16[384,1024]{1,0:T(8,128)(2,1)S(1)} %get-tuple-element.22.dz_ref) | copy-start | bytes 2359300
  212.7 15.8 %copy-start.7 = (f32[16,24576]{1,0:T(8,128)S(1)}, f32[16,24576]{1,0:T(8,128)}, u32[]{:S(2)}) copy-start(f32[16,24576]{1,0:T(8,128)} %w_ref.1) | copy-start | bytes 4718596
  212.7 15.8 %copy-start.10 = (f32[16,24576]{1,0:T(8,128)S(1)}, f32[16,24576]{1,0:T(8,128)}, u32[]{:S(2)}) copy-start(f32[16,24576]{1,0:T(8,128)} %m_ref.1) | copy-start | bytes 4718596
  212.7 15.8 %copy-start.11 = (f32[16,24576]{1,0:T(8,128)S(1)}, f32[16,24576]{1,0:T(8,128)}, u32[]{:S(2)}) copy-start(f32[16,24576]{1,0:T(8,128)} %c_ref.1) | copy-start | bytes 4718596
  215.5 12.4 %collective-permute-start.3 = (bf16[4,24576]{1,0:T(4,128)(2,1)S(1)}, bf16[4,24576]{1,0:T(4,128)(2,1)S(1)}, u32[]{:S(2)}, u32[]{:S(2)}) collective-permute-start(bf16[4,24576]{1,0:T(4,128)(2,1)S(1)} %get-tuple-element.25), channel_id=1, source_target_pairs={{0,1},{1,2},{2,3},{3,0},{4,5},{5,6},{6,7},{7,4},{8,9},{9,10},{10,1... | collective-permute-start | bytes 589832 | tf_op jit(solution)/shard_map/ppermute | solution.py:245
  215.5 12.3 %collective-permute-start.4 = (bf16[4,24576]{1,0:T(4,128)(2,1)S(1)}, bf16[4,24576]{1,0:T(4,128)(2,1)S(1)}, u32[]{:S(2)}, u32[]{:S(2)}) collective-permute-start(bf16[4,24576]{1,0:T(4,128)(2,1)S(1)} %get-tuple-element.26), channel_id=1, source_target_pairs={{0,2},{1,3},{2,0},{3,1},{4,6},{5,7},{6,4},{7,5},{8,10},{9,11},{10,... | collective-permute-start | bytes 589832 | tf_op jit(solution)/shard_map/ppermute | solution.py:245
  217.6 10.9 %collective-permute-start.5 = (bf16[4,24576]{1,0:T(4,128)(2,1)S(1)}, bf16[4,24576]{1,0:T(4,128)(2,1)S(1)}, u32[]{:S(2)}, u32[]{:S(2)}) collective-permute-start(bf16[4,24576]{1,0:T(4,128)(2,1)S(1)} %get-tuple-element.27), channel_id=1, source_target_pairs={{0,3},{1,0},{2,1},{3,2},{4,7},{5,4},{6,5},{7,6},{8,11},{9,8},{10,9... | collective-permute-start | bytes 589832 | tf_op jit(solution)/shard_map/ppermute | solution.py:245
  233.7 14.6 %copy-start.8 = (f32[16,24576]{1,0:T(8,128)}, f32[16,24576]{1,0:T(8,128)S(1)}, u32[]{:S(2)}) copy-start(f32[16,24576]{1,0:T(8,128)S(1)} %get-tuple-element.28.w_ref) | copy-start | bytes 4718596
  234.0 10.8 %collective-permute-start.8 = (bf16[4,24576]{1,0:T(4,128)(2,1)S(1)}, bf16[4,24576]{1,0:T(4,128)(2,1)S(1)}, u32[]{:S(2)}, u32[]{:S(2)}) collective-permute-start(bf16[4,24576]{1,0:T(4,128)(2,1)S(1)} %get-tuple-element.50), channel_id=1, source_target_pairs={{0,3},{1,0},{2,1},{3,2},{4,7},{5,4},{6,5},{7,6},{8,11},{9,8},{10,9... | collective-permute-start | bytes 589832 | tf_op jit(solution)/shard_map/ppermute | solution.py:245
  236.6 9.3 %collective-permute-start.7 = (bf16[4,24576]{1,0:T(4,128)(2,1)S(1)}, bf16[4,24576]{1,0:T(4,128)(2,1)S(1)}, u32[]{:S(2)}, u32[]{:S(2)}) collective-permute-start(bf16[4,24576]{1,0:T(4,128)(2,1)S(1)} %get-tuple-element.51), channel_id=1, source_target_pairs={{0,2},{1,3},{2,0},{3,1},{4,6},{5,7},{6,4},{7,5},{8,10},{9,11},{10,... | collective-permute-start | bytes 589832 | tf_op jit(solution)/shard_map/ppermute | solution.py:245
  236.6 11.7 %collective-permute-start.6 = (bf16[4,24576]{1,0:T(4,128)(2,1)S(1)}, bf16[4,24576]{1,0:T(4,128)(2,1)S(1)}, u32[]{:S(2)}, u32[]{:S(2)}) collective-permute-start(bf16[4,24576]{1,0:T(4,128)(2,1)S(1)} %get-tuple-element.52), channel_id=1, source_target_pairs={{0,1},{1,2},{2,3},{3,0},{4,5},{5,6},{6,7},{7,4},{8,9},{9,10},{10,1... | collective-permute-start | bytes 589832 | tf_op jit(solution)/shard_map/ppermute | solution.py:245
  260.6 82.8 %all-to-all-start.2 = ((bf16[32,96,1024]{2,1,0:T(8,128)(2,1)}), bf16[32,96,1024]{2,1,0:T(8,128)(2,1)}, u32[]{:S(2)}, u32[]{:S(2)}) async-start(bf16[32,96,1024]{2,1,0:T(8,128)(2,1)} %copy-done.3), calls=%async_computation.2 | async-start | bytes 12582912 | tf_op jit(solution)/shard_map/all_to_all | solution.py:263
  361.2 83.0 %all-to-all-start.3 = ((bf16[32,96,1024]{2,1,0:T(8,128)(2,1)}), bf16[32,96,1024]{2,1,0:T(8,128)(2,1)}, u32[]{:S(2)}, u32[]{:S(2)}) async-start(bf16[32,96,1024]{2,1,0:T(8,128)(2,1)} %bitcast.36), calls=%async_computation.3 | async-start | bytes 12582912 | tf_op jit(solution)/shard_map/all_to_all | solution.py:265
  450.6 9.1 %collective-permute-start.9 = (bf16[4,24576]{1,0:T(4,128)(2,1)S(1)}, bf16[4,24576]{1,0:T(4,128)(2,1)S(1)}, u32[]{:S(2)}, u32[]{:S(2)}) collective-permute-start(bf16[4,24576]{1,0:T(4,128)(2,1)S(1)} %get-tuple-element.32), channel_id=1, source_target_pairs={{0,1},{1,2},{2,3},{3,0},{4,5},{5,6},{6,7},{7,4},{8,9},{9,10},{10,1... | collective-permute-start | bytes 589832 | tf_op jit(solution)/shard_map/ppermute | solution.py:245
  450.6 9.0 %collective-permute-start.10 = (bf16[4,24576]{1,0:T(4,128)(2,1)S(1)}, bf16[4,24576]{1,0:T(4,128)(2,1)S(1)}, u32[]{:S(2)}, u32[]{:S(2)}) collective-permute-start(bf16[4,24576]{1,0:T(4,128)(2,1)S(1)} %get-tuple-element.33), channel_id=1, source_target_pairs={{0,2},{1,3},{2,0},{3,1},{4,6},{5,7},{6,4},{7,5},{8,10},{9,11},{10,... | collective-permute-start | bytes 589832 | tf_op jit(solution)/shard_map/ppermute | solution.py:245
  453.0 7.5 %collective-permute-start.11 = (bf16[4,24576]{1,0:T(4,128)(2,1)S(1)}, bf16[4,24576]{1,0:T(4,128)(2,1)S(1)}, u32[]{:S(2)}, u32[]{:S(2)}) collective-permute-start(bf16[4,24576]{1,0:T(4,128)(2,1)S(1)} %get-tuple-element.34), channel_id=1, source_target_pairs={{0,3},{1,0},{2,1},{3,2},{4,7},{5,4},{6,5},{7,6},{8,11},{9,8},{10,9... | collective-permute-start | bytes 589832 | tf_op jit(solution)/shard_map/ppermute | solution.py:245
  453.9 6.7 %copy-start.9 = (f32[16,24576]{1,0:T(8,128)S(1)}, f32[16,24576]{1,0:T(8,128)}, u32[]{:S(2)}) copy-start(f32[16,24576]{1,0:T(8,128)} %copy-done.8) | copy-start | bytes 4718596
  453.9 6.7 %copy-start.13 = (f32[16,24576]{1,0:T(8,128)S(1)}, f32[16,24576]{1,0:T(8,128)}, u32[]{:S(2)}) copy-start(f32[16,24576]{1,0:T(8,128)} %copy-done.12) | copy-start | bytes 4718596
  453.9 6.7 %copy-start.15 = (f32[16,24576]{1,0:T(8,128)S(1)}, f32[16,24576]{1,0:T(8,128)}, u32[]{:S(2)}) copy-start(f32[16,24576]{1,0:T(8,128)} %copy-done.14) | copy-start | bytes 4718596
  (12 other events, 31.1 us)

commit v2 on v0

v2 whole, which is shorter than its diff:
```python
import jax
import jax.numpy as jnp
from jax import lax
from jax.experimental import pallas as pl
from jax.experimental.pallas import tpu as pltpu
from jax.sharding import PartitionSpec as P

D = 2048
FF = 512
ROWS = 384
WIDE = 1024
PIECE = 24
LANES = 128
LIMIT = 58
HALF = 1024

beta_one = 0.9
beta_two = 0.99
rho_scale = 2.0
learn_rate = 0.005
grad_scale = 0.25

F32 = jnp.float32
BF16 = jnp.bfloat16
VMEM = pltpu.VMEM
SMEM = pltpu.SMEM
in_smem = pl.BlockSpec(memory_space=SMEM)
in_hbm = pl.BlockSpec(memory_space=pl.ANY)

NT = (((1,), (1,)), ((), ()))
NN = (((1,), (0,)), ((), ()))


def params(limit_mb):
    return pltpu.CompilerParams(vmem_limit_bytes=limit_mb * 1024 * 1024)


def dot(a, b, dims):
    return lax.dot_general(a, b, dims, preferred_element_type=F32)


def to_rows(values, j, rows_ref):
    for c in range(WIDE // LANES):
        rows_ref[c, pl.ds(j, values.shape[0], PIECE), :] = values[:, c * LANES : (c + 1) * LANES]


def send_rows(ids_ref, rows_ref, bf_ref, out_ref, sem):
    for c in range(WIDE // LANES):
        for e in range(bf_ref.shape[0]):
            piece = rows_ref[c, e * PIECE : (e + 1) * PIECE, :]
            bf_ref[e, :, c * LANES : (c + 1) * LANES] = piece.astype(BF16)

    @pl.loop(0, out_ref.shape[0], unroll=4)
    def _(d):
        pltpu.make_async_copy(bf_ref.at[ids_ref[d]], out_ref.at[d], sem).start()


def row_scratch(experts):
    return VMEM((WIDE // LANES, experts * PIECE, LANES), F32)


def pack_kernel(ids_ref, w_ref, out_ref, w_buf, rows_ref, bf_ref, in_sem, sem):
    read = pltpu.make_async_copy(w_ref, w_buf, in_sem)
    read.start()
    read.wait()
    for j in range(PIECE):
        to_rows(w_buf[:, j * WIDE : (j + 1) * WIDE], j, rows_ref)
    send_rows(ids_ref, rows_ref, bf_ref, out_ref, sem)
    pltpu.make_async_copy(out_ref, out_ref, sem).wait()


def pack(ids, master):
    experts = master.shape[0]
    return pl.pallas_call(
        pack_kernel,
        out_shape=jax.ShapeDtypeStruct(ids.shape + (PIECE, WIDE), BF16),
        in_specs=[in_smem, in_hbm],
        out_specs=in_hbm,
        scratch_shapes=[
            VMEM(master.shape, F32),
            row_scratch(experts),
            VMEM((experts, PIECE, WIDE), BF16),
            pltpu.SemaphoreType.DMA,
            pltpu.SemaphoreType.DMA,
        ],
        compiler_params=params(LIMIT),
        name="pack",
    )(ids, master)


PARTS = 2
DEEP = D // PARTS
TILE = 256


def expert_kernel(x_hbm, xt_hbm, dy_hbm, w_ref, g_ref, dz_out, *scratch):
    x_ref, xt_ref, dy_ref, dz_ref, wgu_ref, wire_ref, wide_ref, wd_ref = scratch[:8]
    z_ref, dh_ref, h_ref, ht_ref, g_buf, in_sem, out_sem, dz_sem = scratch[8:]
    reads = []

    def read(source, target):
        reads.append(pltpu.make_async_copy(source, target, in_sem.at[len(reads)]))
        reads[-1].start()
        return reads[-1]

    down_in = read(w_ref.at[pl.ds(D, 2 * FF), :], wire_ref)
    dy_in = read(dy_hbm, dy_ref)
    x_in = read(x_hbm, x_ref)
    parts = []
    for k in range(PARTS):
        rows = pl.ds(k * DEEP, DEEP)
        parts.append(read(w_ref.at[rows, :], wgu_ref.at[rows, :]))
    xt_in = read(xt_hbm, xt_ref)

    down_in.wait()
    for t in range(2 * FF // TILE):
        down = slice(t * TILE // 2, (t + 1) * TILE // 2)
        for c in range(WIDE // LANES):
            wide_ref[c] = wire_ref[t * TILE : (t + 1) * TILE, c * LANES : (c + 1) * LANES].astype(F32)
            for half in range(2):
                first = half * HALF + c * LANES
                wd_ref[down, first : first + LANES] = wide_ref[c, pl.ds(half, TILE // 2, 2), :].astype(BF16)
    dy_in.wait()
    for n in range(FF // TILE):
        cols = slice(n * TILE, (n + 1) * TILE)
        dh_ref[:, cols] = dot(dy_ref[...], wd_ref[cols, :], NT)
    x_in.wait()
    for k in range(PARTS):
        parts[k].wait()
        rows = slice(k * DEEP, (k + 1) * DEEP)
        for n in range(2 * FF // TILE):
            cols = slice(n * TILE, (n + 1) * TILE)
            part = dot(x_ref[:, rows], wgu_ref[rows, cols], NN)
            z_ref[:, cols] = part if k == 0 else z_ref[:, cols] + part
    for n in range(FF // TILE):
        cols = slice(n * TILE, (n + 1) * TILE)
        ups = slice(FF + n * TILE, FF + (n + 1) * TILE)
        gate, up, dh = z_ref[:, cols], z_ref[:, ups], dh_ref[:, cols]
        sig = jax.nn.sigmoid(gate)
        act = gate * sig
        slope = sig * (1.0 + gate * (1.0 - sig))
        h_ref[:, cols] = (act * up).astype(BF16)
        dz_ref[:, cols] = (dh * up * slope).astype(BF16)
        dz_ref[:, ups] = (dh * act).astype(BF16)
    dz_copy = pltpu.make_async_copy(dz_ref, dz_out, dz_sem)
    dz_copy.start()
    ht_ref[...] = h_ref[...].T
    xt_in.wait()

    @pl.loop(0, D // TILE)
    def _(i):
        rows = pl.ds(pl.multiple_of(i * TILE, TILE), TILE)
        g_buf[rows, :] = dot(xt_ref[rows, :], dz_ref[...], NN).astype(BF16)
        pltpu.make_async_copy(g_buf.at[rows, :], g_ref.at[rows, :], out_sem).start()

    @pl.loop(0, 2 * FF // TILE)
    def _(i):
        rows = pl.ds(pl.multiple_of(i * (TILE // 2), TILE // 2), TILE // 2)
        part = dot(ht_ref[rows, :], dy_ref[...], NN)
        wire = pl.ds(pl.multiple_of(D + i * TILE, TILE), TILE)
        for c in range(WIDE // LANES):
            for half in range(2):
                first = half * HALF + c * LANES
                wide_ref[c, pl.ds(half, TILE // 2, 2), :] = part[:, first : first + LANES]
            g_buf[wire, c * LANES : (c + 1) * LANES] = wide_ref[c].astype(BF16)
        pltpu.make_async_copy(g_buf.at[wire, :], g_ref.at[wire, :], out_sem).start()

    pltpu.make_async_copy(g_buf, g_ref, out_sem).wait()
    dz_copy.wait()


def expert(x, xt, dy, weights):
    return pl.pallas_call(
        expert_kernel,
        out_shape=(
            jax.ShapeDtypeStruct(weights.shape, BF16),
            jax.ShapeDtypeStruct((ROWS, 2 * FF), BF16),
        ),
        in_specs=[in_hbm] * 4,
        out_specs=(in_hbm, in_hbm),
        scratch_shapes=[
            VMEM((ROWS, D), BF16),
            VMEM((D, ROWS), BF16),
            VMEM((ROWS, D), BF16),
            VMEM((ROWS, 2 * FF), BF16),
            VMEM((D, 2 * FF), BF16),
            VMEM((2 * FF, WIDE), BF16),
            VMEM((WIDE // LANES, TILE, LANES), F32),
            VMEM((FF, D), BF16),
            VMEM((ROWS, 2 * FF), F32),
            VMEM((ROWS, FF), F32),
            VMEM((ROWS, FF), BF16),
            VMEM((FF, ROWS), BF16),
            VMEM(weights.shape, BF16),
            pltpu.SemaphoreType.DMA((PARTS + 4,)),
            pltpu.SemaphoreType.DMA,
            pltpu.SemaphoreType.DMA,
        ],
        compiler_params=params(LIMIT),
        name="expert",
    )(x, xt, dy, weights)


def row_grad_kernel(dz_ref, w_ref, out_ref):
    out_ref[...] = dot(dz_ref[...], w_ref[...], NT).astype(BF16)


def row_grad(dz, weights):
    return pl.pallas_call(
        row_grad_kernel,
        grid=(D // TILE,),
        out_shape=jax.ShapeDtypeStruct((ROWS, D), BF16),
        in_specs=[
            pl.BlockSpec((ROWS, 2 * FF), lambda i: (0, 0)),
            pl.BlockSpec((TILE, WIDE), lambda i: (i, 0)),
        ],
        out_specs=pl.BlockSpec((ROWS, TILE), lambda i: (0, i)),
        compiler_params=params(32),
        cost_estimate=pl.CostEstimate(flops=2 * ROWS * D * 2 * FF, bytes_accessed=8 << 20, transcendentals=0),
        name="row_grad",
    )(dz, weights)


def sophia(grads, momentum, curvature, master):
    momentum = beta_one * momentum + (1.0 - beta_one) * grads
    curvature = beta_two * curvature + (1.0 - beta_two) * grads * grads
    master = master - learn_rate * jnp.clip(momentum / (rho_scale * curvature), -1.0, 1.0)
    return momentum, curvature, master


GROUP = 16


def add_slots(ids_ref, in_ref, buf_ref, acc_ref, sems):
    def read(k):
        part = pl.ds(k * GROUP, GROUP)
        return pltpu.make_async_copy(in_ref.at[part], buf_ref.at[part], sems.at[k])

    groups = buf_ref.shape[0] // GROUP
    for k in range(groups):
        read(k).start()
    acc_ref[...] = jnp.zeros_like(acc_ref)

    @pl.loop(0, groups)
    def _(k):
        read(k).wait()

        @pl.loop(0, GROUP, unroll=4)
        def _(i):
            d = k * GROUP + i
            rows = pl.ds(pl.multiple_of(ids_ref[d] * PIECE, 8), PIECE)
            for c in range(WIDE // LANES):
                acc_ref[c, rows, :] += buf_ref[d, :, c * LANES : (c + 1) * LANES].astype(F32)


def from_rows(acc_ref, j, experts):
    parts = [acc_ref[c, pl.ds(j, experts, PIECE), :] for c in range(WIDE // LANES)]
    return jnp.concatenate(parts, axis=1) * grad_scale


def first_update_kernel(ids_ref, next_ref, in_ref, m_ref, c_ref, w_ref, g_ref, out_ref, *scratch):
    buf_ref, acc_ref, rows_ref, bf_ref, m_buf, c_buf, w_buf, g_buf, sems, state_sem, out_sem, g_sem = scratch
    state = [
        pltpu.make_async_copy(a, b, state_sem.at[i])
        for i, (a, b) in enumerate(((m_ref, m_buf), (c_ref, c_buf), (w_ref, w_buf)))
    ]
    for copy in state:
        copy.start()
    add_slots(ids_ref, in_ref, buf_ref, acc_ref, sems)
    for copy in state:
        copy.wait()
    for j in range(PIECE):
        cols = slice(j * WIDE, (j + 1) * WIDE)
        grads = from_rows(acc_ref, j, m_buf.shape[0])
        g_buf[:, cols] = grads
        to_rows(sophia(grads, m_buf[:, cols], c_buf[:, cols], w_buf[:, cols])[2], j, rows_ref)
    send_rows(next_ref, rows_ref, bf_ref, out_ref, out_sem)
    g_copy = pltpu.make_async_copy(g_buf, g_ref, g_sem)
    g_copy.start()
    pltpu.make_async_copy(out_ref, out_ref, out_sem).wait()
    g_copy.wait()


def first_update(ids, next_ids, arrived, momentum, curvature, master):
    experts = master.shape[0]
    dma = pltpu.SemaphoreType.DMA
    return pl.pallas_call(
        first_update_kernel,
        out_shape=(jax.ShapeDtypeStruct(master.shape, F32), jax.ShapeDtypeStruct(arrived.shape, BF16)),
        in_specs=[in_smem] * 2 + [in_hbm] * 4,
        out_specs=(in_hbm,) * 2,
        scratch_shapes=[
            VMEM(arrived.shape, BF16),
            row_scratch(experts),
            row_scratch(experts),
            VMEM((experts, PIECE, WIDE), BF16),
        ]
        + [VMEM(master.shape, F32)] * 4
        + [dma((arrived.shape[0] // GROUP,)), dma((3,)), dma, dma],
        compiler_params=params(LIMIT),
        name="first_update",
    )(ids, next_ids, arrived, momentum, curvature, master)


def last_update_kernel(ids_ref, in_ref, m_ref, c_ref, w_ref, mo_ref, co_ref, wo_ref, *scratch):
    buf_ref, acc_ref, m_buf, c_buf, w_buf, sems, state_sem, out_sem = scratch
    state = [
        pltpu.make_async_copy(a, b, state_sem.at[i])
        for i, (a, b) in enumerate(((m_ref, m_buf), (c_ref, c_buf), (w_ref, w_buf)))
    ]
    for copy in state:
        copy.start()
    add_slots(ids_ref, in_ref, buf_ref, acc_ref, sems)
    for copy in state:
        copy.wait()
    for j in range(PIECE):
        cols = slice(j * WIDE, (j + 1) * WIDE)
        grads = from_rows(acc_ref, j, m_buf.shape[0])
        values = sophia(grads, m_buf[:, cols], c_buf[:, cols], w_buf[:, cols])
        for i, (buf, out) in enumerate(((m_buf, mo_ref), (c_buf, co_ref), (w_buf, wo_ref))):
            buf[:, cols] = values[i]
            pltpu.make_async_copy(buf.at[:, cols], out.at[:, cols], out_sem.at[i]).start()
    for i, (buf, out) in enumerate(((m_buf, mo_ref), (c_buf, co_ref), (w_buf, wo_ref))):
        pltpu.make_async_copy(buf, out, out_sem.at[i]).wait()


def last_update(ids, arrived, momentum, curvature, master):
    experts = master.shape[0]
    dma = pltpu.SemaphoreType.DMA
    return pl.pallas_call(
        last_update_kernel,
        out_shape=(jax.ShapeDtypeStruct(master.shape, F32),) * 3,
        in_specs=[in_smem] + [in_hbm] * 4,
        out_specs=(in_hbm,) * 3,
        scratch_shapes=[VMEM(arrived.shape, BF16), row_scratch(experts)]
        + [VMEM(master.shape, F32)] * 3
        + [dma((arrived.shape[0] // GROUP,)), dma((3,)), dma((3,))],
        compiler_params=params(LIMIT),
        name="last_update",
    )(ids, arrived, momentum, curvature, master)


def exchange(blocks):
    return lax.all_to_all(blocks, ("slot", "grp"), 0, 0, tiled=True)


def body(token_rows, cotangents, row_counts, old_place, new_place, momentum, curvature, master):
    groups = lax.axis_size("grp")
    experts = master.shape[0]
    owners = (jnp.arange(groups, dtype=jnp.int32) * (experts // groups))[None, :]
    old_ids = (old_place + owners).reshape(-1)
    new_ids = (new_place + owners).reshape(-1)

    def slots(step, outgoing):
        arrived = exchange(outgoing)
        weights = arrived.reshape(-1, WIDE)
        live = jnp.arange(ROWS, dtype=jnp.int32)[:, None] < row_counts[step, 0, 0]
        x = token_rows[step, 0, 0]
        dy = jnp.where(live, cotangents[step, 0, 0], jnp.zeros((), BF16))
        grads, dz = expert(x, x.T, dy, weights)
        return exchange(grads.reshape(arrived.shape)), row_grad(dz, weights)

    arrived, first_rows = slots(0, pack(old_ids, master))
    grads, outgoing = first_update(old_ids, new_ids, arrived, momentum, curvature, master)
    state = sophia(grads, momentum, curvature, master)
    arrived, last_rows = slots(1, outgoing)
    state = last_update(new_ids, arrived, *state)
    return (jnp.stack([first_rows, last_rows])[:, None, None], *state)


def solution(mesh):
    tokens = P(None, "slot", "grp", None, None)
    state = P(None, ("slot", "grp"))
    return jax.shard_map(
        body,
        mesh=mesh,
        in_specs=(tokens, tokens, P(None, "slot", "grp"), P(), P(), state, state, state),
        out_specs=(tokens, state, state, state),
        check_vma=False,
    )
```

time: 876 us -> 382 us (0.44); the launches traced: 863 us -> 382 us
  local copies, waits for them, and re-layouts: 181 us -> 9.67 us
  waiting for transfers between devices: 443 us -> 272 us
  other arithmetic: 131 us -> 10.2 us
  matrix products: 72.4 us -> 0 us
  Pallas kernels: 0 us -> 59.5 us
    all_to_all x4, waiting for transfers between devices: 443 us -> 272 us  [exchange(): return lax.all_to_all(blocks, ('slot', 'grp'), 0, 0, tiled=True)]
    all_to_all x6 -> x0, other arithmetic: 107 us -> none  [body(): lax.all_to_all(outgoing, ('slot', 'grp'), split_axis=0, concat_axis=0, ti...]
    unnamed x28 -> x16, local copies, waits for them, and re-layouts: 103 us -> 3.18 us
    dot_general x12 -> x0, matrix products: 72.4 us -> none  [the longest x2 35.9 us: body(): jnp.dot(selector, arrived, precision=lax.Precision.HIGHEST, preferred_ele...]
    pallas_call x0 -> x7, Pallas kernels: none -> 59.5 us  [the longest x2 23.9 us: expert(): pl.pallas_call(expert_kernel, out_shape=(jax.ShapeDtypeStruct(weights.sha...]
    slice x5 -> x2, local copies, waits for them, and re-layouts: 43.8 us -> 4.92 us  [the longest x1 4.34 us: slots(): x = token_rows[step, 0, 0]]
    concatenate x2 -> x0, other arithmetic: 18.6 us -> none  [slot_backward(): jnp.concatenate([grad_gateup.reshape(-1), grad_down.reshape(-1)])]
    dot_general x2 -> x0, local copies, waits for them, and re-layouts: 18.5 us -> none  [slot_backward(): lax.dot_general(rows_one, pre_grad, (((0,), (0,)), ((), ())), preferred_e...]
  transfers between devices with their start and end apart: 4 -> 4, of which waited for: 4 -> 4; matrix products, arithmetic and copies ran while one was open for 1% -> 5% of each run, Pallas kernels for 0% -> 4%
where the time goes in v2:
time: 382 us
  waiting for transfers between devices  272 us (71%)
  Pallas kernels  59.5 us (16%)
  starting transfers between devices  29.4 us (8%)
  other arithmetic  10.2 us (3%)
  local copies, waits for them, and re-layouts  9.67 us (3%)
    all_to_all x4, waiting for transfers between devices, exchange(): return lax.all_to_all(blocks, ('slot', 'grp'), 0, 0, tiled=True)  272 us
    all_to_all x4, starting transfers between devices, exchange(): return lax.all_to_all(blocks, ('slot', 'grp'), 0, 0, tiled=True)  29.4 us
    pallas_call x2, Pallas kernels, expert(): pl.pallas_call(expert_kernel, out_shape=(jax.ShapeDtypeStruct(weights.sha...  23.9 us
    pallas_call x2, Pallas kernels, row_grad(): pl.pallas_call(row_grad_kernel, grid=(D // TILE,), out_shape=jax.ShapeDty...  13.5 us
    pallas_call x1, Pallas kernels, first_update(): pl.pallas_call(first_update_kernel, out_shape=(jax.ShapeDtypeStruct(maste...  9.68 us
  transfers between devices with their start and end apart: 4, of which 4 were waited for; matrix products, arithmetic and copies ran while one was open for 5% of the time, Pallas kernels for 4%

profile of v2, /device:TPU:0, one launch (start us, length us, event | category | flops | bytes accessed | tf_op | source)
XLA Modules:
  0.0 381.6 jit_solution(9210384558673946426)
XLA Ops:
  0.6 0.8 broadcast_add_fusion
  1.5 0.7 reshape.40.ids_ref
  2.2 5.3 %pack.1 = bf16[128,24,1024]{2,1,0:T(8,128)(2,1)} custom-call(s32[128]{0:T(128)} %reshape.40.ids_ref, f32[16,24576]{1,0:T(8,128)} %w_ref.3), custom_call_target="tpu_custom_call" | custom-call | tf_op jit(solution)/shard_map/pack/pallas_call | solution.py:74
  7.5 11.6 %all-to-all-start = ((bf16[128,24,1024]{2,1,0:T(8,128)(2,1)}), bf16[128,24,1024]{2,1,0:T(8,128)(2,1)}, u32[]{:S(2)}, u32[]{:S(2)}) async-start(bf16[128,24,1024]{2,1,0:T(8,128)(2,1)} %pack.1), calls=%async_computation | async-start | bytes 12582912 | tf_op jit(solution)/shard_map/all_to_all | solution.py:344
  19.1 4.3 %fusion.2 = (bf16[1,1,1,384,2048]{4,3,2,1,0:T(8,128)(2,1)S(1)}, bf16[384,2048]{1,0:T(8,128)(2,1)}, bf16[384,2048]{1,0:T(8,128)(2,1)}, bf16[1,1,1,384,2048]{4,3,2,1,0:T(8,128)(2,1)S(1)}) fusion(bf16[2,1,1,384,2048]{4,3,2,1,0:T(8,128)(2,1)} %param.8), kind=kLoop, calls=%fused_computation.14 | loop fusion | bytes 9437184 | tf_op jit(solution)/shard_map/slice | solution.py:358
  23.5 1.6 copy.26
  25.6 1.3 iota_compare_fusion
  26.9 3.8 %bitcast_select_fusion.1 = (bf16[384,2048]{1,0:T(8,128)(2,1)}, bf16[384,2048]{1,0:T(8,128)(2,1)}) fusion(bf16[2,1,1,384,2048]{4,3,2,1,0:T(8,128)(2,1)} %param.9, pred[384]{0:T(512)(128)(4,1)S(1)} %get-tuple-element.44, pred[384]{0:T(512)(128)(4,1)S(1)} %get-tuple-element.43), kind=kLoop, calls=%fused_computation.4 | loop fusion | flops 1572864 | bytes 6292224 | tf_op jit(solution)/shard_map/jit(_where)/select_n | solution.py:359
  30.8 64.3 %all-to-all-done = bf16[128,24,1024]{2,1,0:T(8,128)(2,1)} async-done(((bf16[128,24,1024]{2,1,0:T(8,128)(2,1)}), bf16[128,24,1024]{2,1,0:T(8,128)(2,1)}, u32[]{:S(2)}, u32[]{:S(2)}) %all-to-all-start) | async-done | bytes 6291488 | tf_op jit(solution)/shard_map/all_to_all | solution.py:344
  95.1 11.9 %expert.2 = (bf16[3072,1024]{1,0:T(8,128)(2,1)}, bf16[384,1024]{1,0:T(8,128)(2,1)}) custom-call(bf16[384,2048]{1,0:T(8,128)(2,1)} %get-tuple-element.36.x_hbm, bf16[2048,384]{1,0:T(8,128)(2,1)} %bitcast.30, bf16[384,2048]{1,0:T(8,128)(2,1)} %get-tuple-element.33.dy_hbm, bf16[3072,1024]{1,0:T(8,128)(2,1)} %bitcast.4.w_ref), custom_call_target="tpu_custom_call" | custom-call | tf_op jit(solution)/shard_map/expert/pallas_call | solution.py:173
  107.0 5.8 %all-to-all-start.1 = ((bf16[128,24,1024]{2,1,0:T(8,128)(2,1)}), bf16[128,24,1024]{2,1,0:T(8,128)(2,1)}, u32[]{:S(2)}, u32[]{:S(2)}) async-start(bf16[128,24,1024]{2,1,0:T(8,128)(2,1)} %bitcast.29), calls=%async_computation.1 | async-start | bytes 12582912 | tf_op jit(solution)/shard_map/all_to_all | solution.py:344
  113.6 75.2 %all-to-all-done.1.in_ref = bf16[128,24,1024]{2,1,0:T(8,128)(2,1)} async-done(((bf16[128,24,1024]{2,1,0:T(8,128)(2,1)}), bf16[128,24,1024]{2,1,0:T(8,128)(2,1)}, u32[]{:S(2)}, u32[]{:S(2)}) %all-to-all-start.1) | async-done | bytes 6291488 | tf_op jit(solution)/shard_map/all_to_all | solution.py:344
  188.8 9.7 %first_update.1 = (f32[16,24576]{1,0:T(8,128)}, bf16[128,24,1024]{2,1,0:T(8,128)(2,1)}) custom-call(s32[128]{0:T(128)} %reshape.40.ids_ref, s32[128]{0:T(128)} %reshape.42.next_ref.ids_ref, bf16[128,24,1024]{2,1,0:T(8,128)(2,1)} %all-to-all-done.1.in_ref, f32[16,24576]{1,0:T(8,128)} %m_ref.1, f32[16,24576]{1,0:T(8,128)} %c_ref.1, f32[16,24576]{1,0:T(8,128)} %w_ref.3), custom_call_target="tpu_custom_call" | custom-call | tf_op jit(solution)/shard_map/first_update/pallas_call | solution.py:287
  198.5 6.0 %all-to-all-start.2 = ((bf16[128,24,1024]{2,1,0:T(8,128)(2,1)}), bf16[128,24,1024]{2,1,0:T(8,128)(2,1)}, u32[]{:S(2)}, u32[]{:S(2)}) async-start(bf16[128,24,1024]{2,1,0:T(8,128)(2,1)} %get-tuple-element.15), calls=%async_computation.2 | async-start | bytes 12582912 | tf_op jit(solution)/shard_map/all_to_all | solution.py:344
  204.5 1.6 copy.27
  206.1 74.2 %all-to-all-done.2 = bf16[128,24,1024]{2,1,0:T(8,128)(2,1)} async-done(((bf16[128,24,1024]{2,1,0:T(8,128)(2,1)}), bf16[128,24,1024]{2,1,0:T(8,128)(2,1)}, u32[]{:S(2)}, u32[]{:S(2)}) %all-to-all-start.2) | async-done | bytes 6291488 | tf_op jit(solution)/shard_map/all_to_all | solution.py:344
  280.3 11.9 %expert.3 = (bf16[3072,1024]{1,0:T(8,128)(2,1)}, bf16[384,1024]{1,0:T(8,128)(2,1)}) custom-call(bf16[384,2048]{1,0:T(8,128)(2,1)} %get-tuple-element.37.x_hbm, bf16[2048,384]{1,0:T(8,128)(2,1)} %bitcast.31, bf16[384,2048]{1,0:T(8,128)(2,1)} %get-tuple-element.34.dy_hbm, bf16[3072,1024]{1,0:T(8,128)(2,1)} %bitcast.11.w_ref), custom_call_target="tpu_custom_call" | custom-call | tf_op jit(solution)/shard_map/expert/pallas_call | solution.py:173
  292.3 6.0 %all-to-all-start.3 = ((bf16[128,24,1024]{2,1,0:T(8,128)(2,1)}), bf16[128,24,1024]{2,1,0:T(8,128)(2,1)}, u32[]{:S(2)}, u32[]{:S(2)}) async-start(bf16[128,24,1024]{2,1,0:T(8,128)(2,1)} %bitcast.28), calls=%async_computation.3 | async-start | bytes 12582912 | tf_op jit(solution)/shard_map/all_to_all | solution.py:344
  298.3 7.1 %row_grad.2 = bf16[384,2048]{1,0:T(8,128)(2,1)S(1)} custom-call(bf16[384,1024]{1,0:T(8,128)(2,1)S(1)} %copy-done, bf16[3072,1024]{1,0:T(8,128)(2,1)} %bitcast.4.w_ref), custom_call_target="tpu_custom_call" | custom-call | flops 1610612736 | bytes 8388608 | tf_op jit(solution)/shard_map/row_grad/pallas_call | solution.py:209
  305.4 2.4 multiply_subtract_fusion
  307.8 6.4 %row_grad.3 = bf16[384,2048]{1,0:T(8,128)(2,1)S(1)} custom-call(bf16[384,1024]{1,0:T(8,128)(2,1)S(1)} %copy-done.1, bf16[3072,1024]{1,0:T(8,128)(2,1)} %bitcast.11.w_ref), custom_call_target="tpu_custom_call" | custom-call | flops 1610612736 | bytes 8388608 | tf_op jit(solution)/shard_map/row_grad/pallas_call | solution.py:209
  314.2 1.9 maximum_bitcast_fusion
  316.2 58.0 %all-to-all-done.3.in_ref = bf16[128,24,1024]{2,1,0:T(8,128)(2,1)} async-done(((bf16[128,24,1024]{2,1,0:T(8,128)(2,1)}), bf16[128,24,1024]{2,1,0:T(8,128)(2,1)}, u32[]{:S(2)}, u32[]{:S(2)}) %all-to-all-start.3) | async-done | bytes 6291488 | tf_op jit(solution)/shard_map/all_to_all | solution.py:344
  374.2 7.2 %last_update.1 = (f32[16,24576]{1,0:T(8,128)}, f32[16,24576]{1,0:T(8,128)}, f32[16,24576]{1,0:T(8,128)}) custom-call(s32[128]{0:T(128)} %reshape.42.next_ref.ids_ref, bf16[128,24,1024]{2,1,0:T(8,128)(2,1)} %all-to-all-done.3.in_ref, f32[16,24576]{1,0:T(8,128)} %get-tuple-element.32.m_ref, f32[16,24576]{1,0:T(8,128)} %get-tuple-element.31.c_ref, ...), custom_call_target="tpu_custom_call" | custom-call | tf_op jit(solution)/shard_map/last_update/pallas_call | solution.py:330
  (19 shorter events, 1.5 us)
Async XLA Ops:
  7.5 87.6 %all-to-all-start = ((bf16[128,24,1024]{2,1,0:T(8,128)(2,1)}), bf16[128,24,1024]{2,1,0:T(8,128)(2,1)}, u32[]{:S(2)}, u32[]{:S(2)}) async-start(bf16[128,24,1024]{2,1,0:T(8,128)(2,1)} %pack.1), calls=%async_computation | async-start | bytes 12582912 | tf_op jit(solution)/shard_map/all_to_all | solution.py:344
  23.5 1.6 copy-start.6
  107.0 81.8 %all-to-all-start.1 = ((bf16[128,24,1024]{2,1,0:T(8,128)(2,1)}), bf16[128,24,1024]{2,1,0:T(8,128)(2,1)}, u32[]{:S(2)}, u32[]{:S(2)}) async-start(bf16[128,24,1024]{2,1,0:T(8,128)(2,1)} %bitcast.29), calls=%async_computation.1 | async-start | bytes 12582912 | tf_op jit(solution)/shard_map/all_to_all | solution.py:344
  198.5 81.8 %all-to-all-start.2 = ((bf16[128,24,1024]{2,1,0:T(8,128)(2,1)}), bf16[128,24,1024]{2,1,0:T(8,128)(2,1)}, u32[]{:S(2)}, u32[]{:S(2)}) async-start(bf16[128,24,1024]{2,1,0:T(8,128)(2,1)} %get-tuple-element.15), calls=%async_computation.2 | async-start | bytes 12582912 | tf_op jit(solution)/shard_map/all_to_all | solution.py:344
  292.3 6.0 %copy-start = (bf16[384,1024]{1,0:T(8,128)(2,1)S(1)}, bf16[384,1024]{1,0:T(8,128)(2,1)}, u32[]{:S(2)}) copy-start(bf16[384,1024]{1,0:T(8,128)(2,1)} %get-tuple-element.13.dz_ref) | copy-start | bytes 2359300
  292.3 81.9 %all-to-all-start.3 = ((bf16[128,24,1024]{2,1,0:T(8,128)(2,1)}), bf16[128,24,1024]{2,1,0:T(8,128)(2,1)}, u32[]{:S(2)}, u32[]{:S(2)}) async-start(bf16[128,24,1024]{2,1,0:T(8,128)(2,1)} %bitcast.28), calls=%async_computation.3 | async-start | bytes 12582912 | tf_op jit(solution)/shard_map/all_to_all | solution.py:344
  298.3 7.1 %copy-start.2 = (f32[16,24576]{1,0:T(8,128)S(1)}, f32[16,24576]{1,0:T(8,128)}, u32[]{:S(2)}) copy-start(f32[16,24576]{1,0:T(8,128)} %w_ref.3) | copy-start | bytes 4718596
  298.3 7.1 %copy-start.3 = (f32[16,24576]{1,0:T(8,128)S(1)}, f32[16,24576]{1,0:T(8,128)}, u32[]{:S(2)}) copy-start(f32[16,24576]{1,0:T(8,128)} %m_ref.1) | copy-start | bytes 4718596
  298.3 7.1 %copy-start.4 = (f32[16,24576]{1,0:T(8,128)S(1)}, f32[16,24576]{1,0:T(8,128)}, u32[]{:S(2)}) copy-start(f32[16,24576]{1,0:T(8,128)} %c_ref.1) | copy-start | bytes 4718596
  298.3 7.1 %copy-start.5 = (f32[16,24576]{1,0:T(8,128)S(1)}, f32[16,24576]{1,0:T(8,128)}, u32[]{:S(2)}) copy-start(f32[16,24576]{1,0:T(8,128)} %get-tuple-element.18) | copy-start | bytes 4718596
  305.4 2.4 copy-start.1

commit v3 on v2

v3 whole, which is shorter than its diff:
```python
import jax
import jax.numpy as jnp
from jax import lax
from jax.experimental import pallas as pl
from jax.experimental.pallas import tpu as pltpu
from jax.sharding import PartitionSpec as P

D = 2048
FF = 512
ROWS = 384
WIDE = 1024
PIECE = 24
LANES = 128
EXPERTS = 16
LIMIT = 58
HALF = 1024

beta_one = 0.9
beta_two = 0.99
rho_scale = 2.0
learn_rate = 0.005
grad_scale = 0.25

F32 = jnp.float32
BF16 = jnp.bfloat16
VMEM = pltpu.VMEM
SMEM = pltpu.SMEM
in_smem = pl.BlockSpec(memory_space=SMEM)
in_hbm = pl.BlockSpec(memory_space=pl.ANY)

NT = (((1,), (1,)), ((), ()))
NN = (((1,), (0,)), ((), ()))
TN = (((0,), (0,)), ((), ()))


def params(limit_mb):
    return pltpu.CompilerParams(vmem_limit_bytes=limit_mb * 1024 * 1024)


def dot(a, b, dims):
    return lax.dot_general(a, b, dims, preferred_element_type=F32)


def expert_of(place_ref, d):
    groups = place_ref.shape[0]
    group = lax.rem(d, groups)
    return place_ref[group, lax.div(d, groups)] + group * (EXPERTS // groups)


def to_rows(values, j, rows_ref):
    for c in range(WIDE // LANES):
        rows_ref[c, pl.ds(j, values.shape[0], PIECE), :] = values[:, c * LANES : (c + 1) * LANES]


def send_rows(place_ref, bf_ref, out_ref, sem):
    @pl.loop(0, out_ref.shape[0], unroll=4)
    def _(d):
        pltpu.make_async_copy(bf_ref.at[expert_of(place_ref, d)], out_ref.at[d], sem).start()


ROW_STATE = (WIDE // LANES, EXPERTS * PIECE, LANES)


def pack_kernel(place_ref, w_ref, out_ref, w_buf, rows_ref, bf_ref, in_sem, sem):
    read = pltpu.make_async_copy(w_ref, w_buf, in_sem)
    read.start()
    read.wait()
    for j in range(PIECE):
        to_rows(w_buf[:, j * WIDE : (j + 1) * WIDE], j, rows_ref)
    for c in range(WIDE // LANES):
        for e in range(EXPERTS):
            piece = rows_ref[c, e * PIECE : (e + 1) * PIECE, :]
            bf_ref[e, :, c * LANES : (c + 1) * LANES] = piece.astype(BF16)
    send_rows(place_ref, bf_ref, out_ref, sem)
    pltpu.make_async_copy(out_ref, out_ref, sem).wait()


def pack(place, master):
    return pl.pallas_call(
        pack_kernel,
        out_shape=jax.ShapeDtypeStruct((place.size, PIECE, WIDE), BF16),
        in_specs=[in_smem, in_hbm],
        out_specs=in_hbm,
        scratch_shapes=[
            VMEM(master.shape, F32),
            VMEM(ROW_STATE, F32),
            VMEM((EXPERTS, PIECE, WIDE), BF16),
            pltpu.SemaphoreType.DMA,
            pltpu.SemaphoreType.DMA,
        ],
        compiler_params=params(LIMIT),
        name="pack",
    )(place, master)


def rows_kernel(in_ref, out_ref):
    for j in range(PIECE):
        to_rows(in_ref[:, j * WIDE : (j + 1) * WIDE], j, out_ref)


def rows_of(values):
    return pl.pallas_call(
        rows_kernel,
        out_shape=jax.ShapeDtypeStruct(ROW_STATE, F32),
        compiler_params=params(LIMIT),
        cost_estimate=pl.CostEstimate(flops=values.size, bytes_accessed=8 * values.size, transcendentals=0),
        name="rows_of",
    )(values)


PARTS = 2
DEEP = D // PARTS
TILE = 256


def expert_kernel(x_hbm, dy_hbm, w_ref, g_ref, dz_out, *scratch):
    x_ref, dy_ref, dz_ref, wgu_ref, wire_ref, wide_ref, wd_ref = scratch[:7]
    z_ref, dh_ref, h_ref, ht_ref, g_buf, in_sem, out_sem, dz_sem = scratch[7:]
    reads = []

    def read(source, target):
        reads.append(pltpu.make_async_copy(source, target, in_sem.at[len(reads)]))
        reads[-1].start()
        return reads[-1]

    down_in = read(w_ref.at[pl.ds(D, 2 * FF), :], wire_ref)
    dy_in = read(dy_hbm, dy_ref)
    x_in = read(x_hbm, x_ref)
    parts = []
    for k in range(PARTS):
        rows = pl.ds(k * DEEP, DEEP)
        parts.append(read(w_ref.at[rows, :], wgu_ref.at[rows, :]))

    down_in.wait()
    for t in range(2 * FF // TILE):
        down = slice(t * TILE // 2, (t + 1) * TILE // 2)
        for c in range(WIDE // LANES):
            wide_ref[c] = wire_ref[t * TILE : (t + 1) * TILE, c * LANES : (c + 1) * LANES].astype(F32)
            for half in range(2):
                first = half * HALF + c * LANES
                wd_ref[down, first : first + LANES] = wide_ref[c, pl.ds(half, TILE // 2, 2), :].astype(BF16)
    dy_in.wait()
    for n in range(FF // TILE):
        cols = slice(n * TILE, (n + 1) * TILE)
        dh_ref[:, cols] = dot(dy_ref[...], wd_ref[cols, :], NT)
    x_in.wait()
    for k in range(PARTS):
        parts[k].wait()
        rows = slice(k * DEEP, (k + 1) * DEEP)
        for n in range(FF // TILE):
            cols = slice(n * TILE, (n + 1) * TILE)
            ups = slice(FF + n * TILE, FF + (n + 1) * TILE)
            gate = dot(x_ref[:, rows], wgu_ref[rows, cols], NN)
            up = dot(x_ref[:, rows], wgu_ref[rows, ups], NN)
            if k > 0:
                gate, up = gate + z_ref[:, cols], up + z_ref[:, ups]
            if k < PARTS - 1:
                z_ref[:, cols], z_ref[:, ups] = gate, up
                continue
            dh = dh_ref[:, cols]
            sig = jax.nn.sigmoid(gate)
            act = gate * sig
            slope = sig * (1.0 + gate * (1.0 - sig))
            h_ref[:, cols] = (act * up).astype(BF16)
            dz_ref[:, cols] = (dh * up * slope).astype(BF16)
            dz_ref[:, ups] = (dh * act).astype(BF16)
    dz_copy = pltpu.make_async_copy(dz_ref, dz_out, dz_sem)
    dz_copy.start()
    ht_ref[...] = h_ref[...].T

    for i in range(D // TILE):
        rows = slice(i * TILE, (i + 1) * TILE)
        g_buf[rows, :] = dot(x_ref[:, rows], dz_ref[...], TN).astype(BF16)
        pltpu.make_async_copy(g_buf.at[pl.ds(i * TILE, TILE), :], g_ref.at[pl.ds(i * TILE, TILE), :], out_sem).start()

    @pl.loop(0, 2 * FF // TILE, unroll=True)
    def _(i):
        rows = pl.ds(pl.multiple_of(i * (TILE // 2), TILE // 2), TILE // 2)
        part = dot(ht_ref[rows, :], dy_ref[...], NN)
        wire = pl.ds(pl.multiple_of(D + i * TILE, TILE), TILE)
        for c in range(WIDE // LANES):
            for half in range(2):
                first = half * HALF + c * LANES
                wide_ref[c, pl.ds(half, TILE // 2, 2), :] = part[:, first : first + LANES]
            g_buf[wire, c * LANES : (c + 1) * LANES] = wide_ref[c].astype(BF16)
        pltpu.make_async_copy(g_buf.at[wire, :], g_ref.at[wire, :], out_sem).start()

    pltpu.make_async_copy(g_buf, g_ref, out_sem).wait()
    dz_copy.wait()


def expert(x, dy, weights):
    return pl.pallas_call(
        expert_kernel,
        out_shape=(
            jax.ShapeDtypeStruct(weights.shape, BF16),
            jax.ShapeDtypeStruct((ROWS, 2 * FF), BF16),
        ),
        in_specs=[in_hbm] * 3,
        out_specs=(in_hbm, in_hbm),
        scratch_shapes=[
            VMEM((ROWS, D), BF16),
            VMEM((ROWS, D), BF16),
            VMEM((ROWS, 2 * FF), BF16),
            VMEM((D, 2 * FF), BF16),
            VMEM((2 * FF, WIDE), BF16),
            VMEM((WIDE // LANES, TILE, LANES), F32),
            VMEM((FF, D), BF16),
            VMEM((ROWS, 2 * FF), F32),
            VMEM((ROWS, FF), F32),
            VMEM((ROWS, FF), BF16),
            VMEM((FF, ROWS), BF16),
            VMEM(weights.shape, BF16),
            pltpu.SemaphoreType.DMA((PARTS + 3,)),
            pltpu.SemaphoreType.DMA,
            pltpu.SemaphoreType.DMA,
        ],
        compiler_params=params(LIMIT),
        name="expert",
    )(x, dy, weights)


def row_grad_kernel(dz_ref, w_ref, out_ref):
    out_ref[...] = dot(dz_ref[...], w_ref[...], NT).astype(BF16)


def row_grad(dz, weights):
    return pl.pallas_call(
        row_grad_kernel,
        grid=(D // TILE,),
        out_shape=jax.ShapeDtypeStruct((ROWS, D), BF16),
        in_specs=[
            pl.BlockSpec((ROWS, 2 * FF), lambda i: (0, 0)),
            pl.BlockSpec((TILE, WIDE), lambda i: (i, 0)),
        ],
        out_specs=pl.BlockSpec((ROWS, TILE), lambda i: (0, i)),
        compiler_params=params(32),
        cost_estimate=pl.CostEstimate(flops=2 * ROWS * D * 2 * FF, bytes_accessed=8 << 20, transcendentals=0),
        name="row_grad",
    )(dz, weights)


def sophia(grads, momentum, curvature, master):
    momentum = beta_one * momentum + (1.0 - beta_one) * grads
    curvature = beta_two * curvature + (1.0 - beta_two) * grads * grads
    master = master - learn_rate * jnp.clip(momentum / (rho_scale * curvature), -1.0, 1.0)
    return momentum, curvature, master


GROUP = 16
UNROLL = 2


def add_slots(place_ref, in_ref, buf_ref, acc_ref, sems):
    def read(k):
        part = pl.ds(k * GROUP, GROUP)
        return pltpu.make_async_copy(in_ref.at[part], buf_ref.at[part], sems.at[k])

    groups = buf_ref.shape[0] // GROUP
    for k in range(groups):
        read(k).start()
    for acc in acc_ref:
        acc[...] = jnp.zeros_like(acc)

    @pl.loop(0, groups)
    def _(k):
        read(k).wait()

        @pl.loop(0, GROUP, step=2 * UNROLL)
        def _(i):
            for u in range(2 * UNROLL):
                d = k * GROUP + i + u
                acc = acc_ref[u % 2]
                rows = pl.ds(pl.multiple_of(expert_of(place_ref, d) * PIECE, 8), PIECE)
                for c in range(WIDE // LANES):
                    acc[c, rows, :] += buf_ref[d, :, c * LANES : (c + 1) * LANES].astype(F32)


def from_rows(acc_ref, j):
    parts = [acc_ref[c, pl.ds(j, EXPERTS, PIECE), :] for c in range(WIDE // LANES)]
    return jnp.concatenate(parts, axis=1)


def first_update_kernel(place_ref, next_ref, in_ref, m_ref, c_ref, w_ref, g_ref, out_ref, *scratch):
    buf_ref, even_ref, odd_ref, bf_ref, m_buf, c_buf, w_buf, sems, state_sem, out_sem, g_sem = scratch
    state = [
        pltpu.make_async_copy(a, b, state_sem.at[i])
        for i, (a, b) in enumerate(((m_ref, m_buf), (c_ref, c_buf), (w_ref, w_buf)))
    ]
    for copy in state:
        copy.start()
    add_slots(place_ref, in_ref, buf_ref, (even_ref, odd_ref), sems)
    for copy in state:
        copy.wait()

    @pl.loop(0, EXPERTS)
    def _(e):
        rows = pl.ds(pl.multiple_of(e * PIECE, 8), PIECE)
        for c in range(WIDE // LANES):
            grads = (even_ref[c, rows, :] + odd_ref[c, rows, :]) * grad_scale
            even_ref[c, rows, :] = grads
            master = sophia(grads, m_buf[c, rows, :], c_buf[c, rows, :], w_buf[c, rows, :])[2]
            bf_ref[e, :, c * LANES : (c + 1) * LANES] = master.astype(BF16)

    send_rows(next_ref, bf_ref, out_ref, out_sem)
    g_copy = pltpu.make_async_copy(even_ref, g_ref, g_sem)
    g_copy.start()
    pltpu.make_async_copy(out_ref, out_ref, out_sem).wait()
    g_copy.wait()


def first_update(place, next_place, arrived, momentum, curvature, master):
    dma = pltpu.SemaphoreType.DMA
    return pl.pallas_call(
        first_update_kernel,
        out_shape=(jax.ShapeDtypeStruct(ROW_STATE, F32), jax.ShapeDtypeStruct(arrived.shape, BF16)),
        in_specs=[in_smem] * 2 + [in_hbm] * 4,
        out_specs=(in_hbm,) * 2,
        scratch_shapes=[VMEM(arrived.shape, BF16)]
        + [VMEM(ROW_STATE, F32)] * 2
        + [VMEM((EXPERTS, PIECE, WIDE), BF16)]
        + [VMEM(ROW_STATE, F32)] * 3
        + [dma((arrived.shape[0] // GROUP,)), dma((3,)), dma, dma],
        compiler_params=params(LIMIT),
        name="first_update",
    )(place, next_place, arrived, momentum, curvature, master)


def first_state_kernel(g_ref, m_ref, c_ref, w_ref, mo_ref, co_ref, wo_ref):
    for j in range(PIECE):
        cols = slice(j * WIDE, (j + 1) * WIDE)
        values = sophia(from_rows(g_ref, j), m_ref[:, cols], c_ref[:, cols], w_ref[:, cols])
        mo_ref[:, cols], co_ref[:, cols], wo_ref[:, cols] = values


def first_state(grads, momentum, curvature, master):
    return pl.pallas_call(
        first_state_kernel,
        out_shape=(jax.ShapeDtypeStruct(master.shape, F32),) * 3,
        compiler_params=params(LIMIT),
        cost_estimate=pl.CostEstimate(flops=9 * master.size, bytes_accessed=28 * master.size, transcendentals=0),
        name="first_state",
    )(grads, momentum, curvature, master)


def last_update_kernel(place_ref, in_ref, m_ref, c_ref, w_ref, mo_ref, co_ref, wo_ref, *scratch):
    buf_ref, even_ref, odd_ref, m_buf, c_buf, w_buf, sems, state_sem, out_sem = scratch
    state = [
        pltpu.make_async_copy(a, b, state_sem.at[i])
        for i, (a, b) in enumerate(((m_ref, m_buf), (c_ref, c_buf), (w_ref, w_buf)))
    ]
    for copy in state:
        copy.start()
    add_slots(place_ref, in_ref, buf_ref, (even_ref, odd_ref), sems)
    for copy in state:
        copy.wait()
    for j in range(PIECE):
        cols = slice(j * WIDE, (j + 1) * WIDE)
        grads = (from_rows(even_ref, j) + from_rows(odd_ref, j)) * grad_scale
        values = sophia(grads, m_buf[:, cols], c_buf[:, cols], w_buf[:, cols])
        for i, (buf, out) in enumerate(((m_buf, mo_ref), (c_buf, co_ref), (w_buf, wo_ref))):
            buf[:, cols] = values[i]
            pltpu.make_async_copy(buf.at[:, cols], out.at[:, cols], out_sem.at[i]).start()
    for i, (buf, out) in enumerate(((m_buf, mo_ref), (c_buf, co_ref), (w_buf, wo_ref))):
        pltpu.make_async_copy(buf, out, out_sem.at[i]).wait()


def last_update(place, arrived, momentum, curvature, master):
    dma = pltpu.SemaphoreType.DMA
    return pl.pallas_call(
        last_update_kernel,
        out_shape=(jax.ShapeDtypeStruct(master.shape, F32),) * 3,
        in_specs=[in_smem] + [in_hbm] * 4,
        out_specs=(in_hbm,) * 3,
        scratch_shapes=[VMEM(arrived.shape, BF16)]
        + [VMEM(ROW_STATE, F32)] * 2
        + [VMEM(master.shape, F32)] * 3
        + [dma((arrived.shape[0] // GROUP,)), dma((3,)), dma((3,))],
        compiler_params=params(LIMIT),
        name="last_update",
    )(place, arrived, momentum, curvature, master)


def exchange(blocks):
    return lax.all_to_all(blocks, ("slot", "grp"), 0, 0, tiled=True)


def body(token_rows, cotangents, row_counts, old_place, new_place, momentum, curvature, master):
    old_place, new_place = old_place.T, new_place.T

    def slots(step, outgoing):
        arrived = exchange(outgoing)
        weights = arrived.reshape(-1, WIDE)
        live = jnp.arange(ROWS, dtype=jnp.int32)[:, None] < row_counts[step, 0, 0]
        dy = jnp.where(live, cotangents[step, 0, 0], jnp.zeros((), BF16))
        grads, dz = expert(token_rows[step, 0, 0], dy, weights)
        return exchange(grads.reshape(arrived.shape)), row_grad(dz, weights)

    arrived, first_rows = slots(0, pack(old_place, master))
    state = [rows_of(v) for v in (momentum, curvature, master)]
    grads, outgoing = first_update(old_place, new_place, arrived, *state)
    arrived, last_rows = slots(1, outgoing)
    state = first_state(grads, momentum, curvature, master)
    state = last_update(new_place, arrived, *state)
    return (jnp.stack([first_rows, last_rows])[:, None, None], *state)


def solution(mesh):
    tokens = P(None, "slot", "grp", None, None)
    state = P(None, ("slot", "grp"))
    return jax.shard_map(
        body,
        mesh=mesh,
        in_specs=(tokens, tokens, P(None, "slot", "grp"), P(), P(), state, state, state),
        out_specs=(tokens, state, state, state),
        check_vma=False,
    )
```

time: 382 us -> 375 us (0.982)
  blocking collectives: 0 us -> 80.5 us
  waiting for transfers between devices: 272 us -> 192 us
  Pallas kernels: 59.5 us -> 66.4 us
  starting transfers between devices: 29.4 us -> 23.4 us
  other arithmetic: 10.2 us -> 5.18 us
    all_to_all x0 -> x1, blocking collectives: none -> 80.5 us  [exchange(): return lax.all_to_all(blocks, ('slot', 'grp'), 0, 0, tiled=True)]
    all_to_all x4 -> x3, waiting for transfers between devices: 272 us -> 192 us  [exchange(): return lax.all_to_all(blocks, ('slot', 'grp'), 0, 0, tiled=True)]
    pallas_call x2 -> x6, Pallas kernels: 15 us -> 29.3 us  [the longest x1 9.3 us: first_update(): pl.pallas_call(first_update_kernel, out_shape=(jax.ShapeDtypeStruct(ROW_S...]
    all_to_all x4 -> x3, starting transfers between devices: 29.4 us -> 23.4 us  [exchange(): return lax.all_to_all(blocks, ('slot', 'grp'), 0, 0, tiled=True)]
    slice x1 -> x0, local copies, waits for them, and re-layouts: 4.34 us -> none  [slots(): x = token_rows[step, 0, 0]]
    pallas_call x2, Pallas kernels: 23.9 us -> 20 us  [expert(): pl.pallas_call(expert_kernel, out_shape=(jax.ShapeDtypeStruct(weights.sha...]
  transfers between devices with their start and end apart: 4 -> 3, of which waited for: 4 -> 3; matrix products, arithmetic and copies ran while one was open for 5% -> 2% of each run, Pallas kernels for 4% -> 7%
where the time goes in v3:
time: 375 us
  waiting for transfers between devices  192 us (51%)
  blocking collectives  80.5 us (21%)
  Pallas kernels  66.4 us (18%)
  starting transfers between devices  23.4 us (6%)
  local copies, waits for them, and re-layouts  6.41 us (2%)
  other arithmetic  5.18 us (1%)
    all_to_all x3, waiting for transfers between devices, exchange(): return lax.all_to_all(blocks, ('slot', 'grp'), 0, 0, tiled=True)  192 us
    all_to_all x1, blocking collectives, exchange(): return lax.all_to_all(blocks, ('slot', 'grp'), 0, 0, tiled=True)  80.5 us
    all_to_all x3, starting transfers between devices, exchange(): return lax.all_to_all(blocks, ('slot', 'grp'), 0, 0, tiled=True)  23.4 us
    pallas_call x2, Pallas kernels, expert(): pl.pallas_call(expert_kernel, out_shape=(jax.ShapeDtypeStruct(weights.sha...  20 us
    pallas_call x2, Pallas kernels, row_grad(): pl.pallas_call(row_grad_kernel, grid=(D // TILE,), out_shape=jax.ShapeDty...  9.92 us
    pallas_call x1, Pallas kernels, first_update(): pl.pallas_call(first_update_kernel, out_shape=(jax.ShapeDtypeStruct(ROW_S...  9.3 us
    pallas_call x3, Pallas kernels, rows_of(): pl.pallas_call(rows_kernel, out_shape=jax.ShapeDtypeStruct(ROW_STATE, F32...  8.91 us
  transfers between devices with their start and end apart: 3, of which 3 were waited for; matrix products, arithmetic and copies ran while one was open for 2% of the time, Pallas kernels for 7%

profile of v3, /device:TPU:0, one launch (start us, length us, event | category | flops | bytes accessed | tf_op | source)
XLA Modules:
  0.0 374.5 jit_solution(18096152770416579930)
XLA Ops:
  0.6 5.3 %pack.1 = bf16[128,24,1024]{2,1,0:T(8,128)(2,1)} custom-call(s32[4,32]{1,0:T(4,128)} %bitcast.28, f32[16,24576]{1,0:T(8,128)} %w_ref.3), custom_call_target="tpu_custom_call" | custom-call | tf_op jit(solution)/shard_map/pack/pallas_call | solution.py:79
  6.0 11.6 %all-to-all-start = ((bf16[128,24,1024]{2,1,0:T(8,128)(2,1)}), bf16[128,24,1024]{2,1,0:T(8,128)(2,1)}, u32[]{:S(2)}, u32[]{:S(2)}) async-start(bf16[128,24,1024]{2,1,0:T(8,128)(2,1)} %pack.1), calls=%async_computation | async-start | bytes 12582912 | tf_op jit(solution)/shard_map/all_to_all | solution.py:385
  18.2 1.3 iota_compare_fusion
  19.5 1.9 slice_bitcast_fusion.1
  21.4 1.1 copy-done.4
  22.6 1.9 bitcast_select_fusion.1
  24.5 69.1 %all-to-all-done = bf16[128,24,1024]{2,1,0:T(8,128)(2,1)} async-done(((bf16[128,24,1024]{2,1,0:T(8,128)(2,1)}), bf16[128,24,1024]{2,1,0:T(8,128)(2,1)}, u32[]{:S(2)}, u32[]{:S(2)}) %all-to-all-start) | async-done | bytes 6291488 | tf_op jit(solution)/shard_map/all_to_all | solution.py:385
  93.6 10.0 %expert.2 = (bf16[3072,1024]{1,0:T(8,128)(2,1)}, bf16[384,1024]{1,0:T(8,128)(2,1)}) custom-call(bf16[384,2048]{1,0:T(8,128)(2,1)} %get-tuple-element.34.x_hbm, bf16[384,2048]{1,0:T(8,128)(2,1)} %get-tuple-element.32.dy_hbm, bf16[3072,1024]{1,0:T(8,128)(2,1)} %bitcast.4.w_ref), custom_call_target="tpu_custom_call" | custom-call | tf_op jit(solution)/shard_map/expert/pallas_call | solution.py:193
  103.6 5.8 %all-to-all-start.1 = ((bf16[128,24,1024]{2,1,0:T(8,128)(2,1)}), bf16[128,24,1024]{2,1,0:T(8,128)(2,1)}, u32[]{:S(2)}, u32[]{:S(2)}) async-start(bf16[128,24,1024]{2,1,0:T(8,128)(2,1)} %bitcast.27), calls=%async_computation.1 | async-start | bytes 12582912 | tf_op jit(solution)/shard_map/all_to_all | solution.py:385
  109.4 3.0 rows_of.5.w_ref
  112.4 3.0 rows_of.3.m_ref
  115.4 3.0 rows_of.4.c_ref
  118.3 67.1 %all-to-all-done.1.in_ref = bf16[128,24,1024]{2,1,0:T(8,128)(2,1)} async-done(((bf16[128,24,1024]{2,1,0:T(8,128)(2,1)}), bf16[128,24,1024]{2,1,0:T(8,128)(2,1)}, u32[]{:S(2)}, u32[]{:S(2)}) %all-to-all-start.1) | async-done | bytes 6291488 | tf_op jit(solution)/shard_map/all_to_all | solution.py:385
  185.4 9.3 %first_update.1 = (f32[8,384,128]{2,1,0:T(8,128)}, bf16[128,24,1024]{2,1,0:T(8,128)(2,1)}) custom-call(s32[4,32]{1,0:T(4,128)} %bitcast.29, s32[4,32]{1,0:T(4,128)} %bitcast.30, bf16[128,24,1024]{2,1,0:T(8,128)(2,1)} %all-to-all-done.1.in_ref, f32[8,384,128]{2,1,0:T(8,128)} %rows_of.3.m_ref, f32[8,384,128]{2,1,0:T(8,128)} %rows_of.4.c_ref, ...), custom_call_target="tpu_custom_call" | custom-call | tf_op jit(solution)/shard_map/first_update/pallas_call | solution.py:314
  194.7 80.5 %all_to_all.20 = bf16[128,24,1024]{2,1,0:T(8,128)(2,1)} all-to-all(bf16[128,24,1024]{2,1,0:T(8,128)(2,1)} %get-tuple-element.18), channel_id=1, replica_groups=mesh['slot'=32,'grp'=4] {'slot','grp'}, dimensions={0} | all-to-all | bytes 12582912 | tf_op jit(solution)/shard_map/all_to_all | solution.py:385
  275.1 10.0 %expert.3 = (bf16[3072,1024]{1,0:T(8,128)(2,1)}, bf16[384,1024]{1,0:T(8,128)(2,1)}) custom-call(bf16[384,2048]{1,0:T(8,128)(2,1)} %get-tuple-element.35.x_hbm, bf16[384,2048]{1,0:T(8,128)(2,1)} %get-tuple-element.33.dy_hbm, bf16[3072,1024]{1,0:T(8,128)(2,1)} %bitcast.22), custom_call_target="tpu_custom_call" | custom-call | tf_op jit(solution)/shard_map/expert/pallas_call | solution.py:193
  285.2 6.0 %all-to-all-start.3 = ((bf16[128,24,1024]{2,1,0:T(8,128)(2,1)}), bf16[128,24,1024]{2,1,0:T(8,128)(2,1)}, u32[]{:S(2)}, u32[]{:S(2)}) async-start(bf16[128,24,1024]{2,1,0:T(8,128)(2,1)} %bitcast.26), calls=%async_computation.3 | async-start | bytes 12582912 | tf_op jit(solution)/shard_map/all_to_all | solution.py:385
  291.1 6.4 %row_grad.2 = bf16[384,2048]{1,0:T(8,128)(2,1)S(1)} custom-call(bf16[384,1024]{1,0:T(8,128)(2,1)S(1)} %copy-done.1, bf16[3072,1024]{1,0:T(8,128)(2,1)} %bitcast.4.w_ref), custom_call_target="tpu_custom_call" | custom-call | flops 1610612736 | bytes 8388608 | tf_op jit(solution)/shard_map/row_grad/pallas_call | solution.py:228
  297.6 5.7 %first_state.1 = (f32[16,24576]{1,0:T(8,128)}, f32[16,24576]{1,0:T(8,128)}, f32[16,24576]{1,0:T(8,128)}) custom-call(f32[8,384,128]{2,1,0:T(8,128)} %get-tuple-element.21.g_ref, f32[16,24576]{1,0:T(8,128)} %m_ref.1, f32[16,24576]{1,0:T(8,128)} %c_ref.1, f32[16,24576]{1,0:T(8,128)} %w_ref.3), custom_call_target="tpu_custom_call" | custom-call | flops 3538944 | bytes 11010048 | tf_op jit(solution)/shard_map/first_state/pallas_call | solution.py:337
  303.3 2.8 copy-done
  306.1 3.5 row_grad.3
  309.6 1.9 maximum_bitcast_fusion
  311.5 55.6 %all-to-all-done.3.in_ref = bf16[128,24,1024]{2,1,0:T(8,128)(2,1)} async-done(((bf16[128,24,1024]{2,1,0:T(8,128)(2,1)}), bf16[128,24,1024]{2,1,0:T(8,128)(2,1)}, u32[]{:S(2)}, u32[]{:S(2)}) %all-to-all-start.3) | async-done | bytes 6291488 | tf_op jit(solution)/shard_map/all_to_all | solution.py:385
  367.1 7.3 %last_update.1 = (f32[16,24576]{1,0:T(8,128)}, f32[16,24576]{1,0:T(8,128)}, f32[16,24576]{1,0:T(8,128)}) custom-call(s32[4,32]{1,0:T(4,128)} %bitcast.31, bf16[128,24,1024]{2,1,0:T(8,128)(2,1)} %all-to-all-done.3.in_ref, f32[16,24576]{1,0:T(8,128)} %get-tuple-element.22.m_ref, f32[16,24576]{1,0:T(8,128)} %get-tuple-element.23.c_ref, ...), custom_call_target="tpu_custom_call" | custom-call | tf_op jit(solution)/shard_map/last_update/pallas_call | solution.py:370
  (11 shorter events, 0.6 us)
Async XLA Ops:
  6.0 11.7 %copy-start.5 = (s32[2,1,1]{0,2,1:T(1,128)S(1)}, s32[2,1,1]{0,2,1:T(1,128)}, u32[]{:S(2)}) copy-start(s32[2,1,1]{0,2,1:T(1,128)} %param.10) | copy-start | bytes 28
  6.0 13.5 %copy-start.3 = (bf16[2,1,1,384,2048]{4,3,2,1,0:T(8,128)(2,1)S(1)}, bf16[2,1,1,384,2048]{4,3,2,1,0:T(8,128)(2,1)}, u32[]{:S(2)}) copy-start(bf16[2,1,1,384,2048]{4,3,2,1,0:T(8,128)(2,1)} %param.8) | copy-start | bytes 9437188
  6.0 87.6 %all-to-all-start = ((bf16[128,24,1024]{2,1,0:T(8,128)(2,1)}), bf16[128,24,1024]{2,1,0:T(8,128)(2,1)}, u32[]{:S(2)}, u32[]{:S(2)}) async-start(bf16[128,24,1024]{2,1,0:T(8,128)(2,1)} %pack.1), calls=%async_computation | async-start | bytes 12582912 | tf_op jit(solution)/shard_map/all_to_all | solution.py:385
  19.5 3.0 copy-start.4
  103.6 81.8 %all-to-all-start.1 = ((bf16[128,24,1024]{2,1,0:T(8,128)(2,1)}), bf16[128,24,1024]{2,1,0:T(8,128)(2,1)}, u32[]{:S(2)}, u32[]{:S(2)}) async-start(bf16[128,24,1024]{2,1,0:T(8,128)(2,1)} %bitcast.27), calls=%async_computation.1 | async-start | bytes 12582912 | tf_op jit(solution)/shard_map/all_to_all | solution.py:385
  285.1 6.0 %copy-start.1 = (bf16[384,1024]{1,0:T(8,128)(2,1)S(1)}, bf16[384,1024]{1,0:T(8,128)(2,1)}, u32[]{:S(2)}) copy-start(bf16[384,1024]{1,0:T(8,128)(2,1)} %get-tuple-element.16.dz_ref) | copy-start | bytes 2359300
  285.2 81.9 %all-to-all-start.3 = ((bf16[128,24,1024]{2,1,0:T(8,128)(2,1)}), bf16[128,24,1024]{2,1,0:T(8,128)(2,1)}, u32[]{:S(2)}, u32[]{:S(2)}) async-start(bf16[128,24,1024]{2,1,0:T(8,128)(2,1)} %bitcast.26), calls=%async_computation.3 | async-start | bytes 12582912 | tf_op jit(solution)/shard_map/all_to_all | solution.py:385
  297.6 5.7 %copy-start.2 = (bf16[384,1024]{1,0:T(8,128)(2,1)S(1)}, bf16[384,1024]{1,0:T(8,128)(2,1)}, u32[]{:S(2)}) copy-start(bf16[384,1024]{1,0:T(8,128)(2,1)} %get-tuple-element.19.dz_ref) | copy-start | bytes 2359300
  303.3 2.8 copy-start

commit v4 on v3

--- a/solution.py
+++ b/solution.py
@@ -1,3 +1,5 @@
+import functools
+
 import jax
 import jax.numpy as jnp
 from jax import lax
@@ -25,7 +27,6 @@
 BF16 = jnp.bfloat16
 VMEM = pltpu.VMEM
 SMEM = pltpu.SMEM
-in_smem = pl.BlockSpec(memory_space=SMEM)
 in_hbm = pl.BlockSpec(memory_space=pl.ANY)
 
 NT = (((1,), (1,)), ((), ()))
@@ -52,39 +53,63 @@
         rows_ref[c, pl.ds(j, values.shape[0], PIECE), :] = values[:, c * LANES : (c + 1) * LANES]
 
 
-def send_rows(place_ref, bf_ref, out_ref, sem):
-    @pl.loop(0, out_ref.shape[0], unroll=4)
-    def _(d):
-        pltpu.make_async_copy(bf_ref.at[expert_of(place_ref, d)], out_ref.at[d], sem).start()
-
-
-ROW_STATE = (WIDE // LANES, EXPERTS * PIECE, LANES)
-
-
-def pack_kernel(place_ref, w_ref, out_ref, w_buf, rows_ref, bf_ref, in_sem, sem):
-    read = pltpu.make_async_copy(w_ref, w_buf, in_sem)
-    read.start()
-    read.wait()
-    for j in range(PIECE):
-        to_rows(w_buf[:, j * WIDE : (j + 1) * WIDE], j, rows_ref)
+BATCH = 4
+GROUP = 8
+
+
+def round_rows(rows_ref, bf_ref):
     for c in range(WIDE // LANES):
         for e in range(EXPERTS):
             piece = rows_ref[c, e * PIECE : (e + 1) * PIECE, :]
             bf_ref[e, :, c * LANES : (c + 1) * LANES] = piece.astype(BF16)
-    send_rows(place_ref, bf_ref, out_ref, sem)
-    pltpu.make_async_copy(out_ref, out_ref, sem).wait()
+
+
+def send_rows(place_ref, bf_ref, all_ref, out_ref, sem):
+    @pl.loop(0, all_ref.shape[0] // GROUP)
+    def _(k):
+        @pl.loop(0, GROUP, unroll=8)
+        def _(i):
+            d = k * GROUP + i
+            all_ref[d] = bf_ref[expert_of(place_ref, d)]
+
+        part = pl.ds(k * GROUP, GROUP)
+        pltpu.make_async_copy(all_ref.at[part], out_ref.at[part], sem).start()
+
+
+ROW_STATE = (WIDE // LANES, EXPERTS * PIECE, LANES)
+
+
+def pack_kernel(place_hbm, w_ref, out_ref, w_buf, rows_ref, bf_ref, all_ref, place_ref, in_sem, sem, place_sem):
+    reads = []
+    for k in range(PIECE // BATCH):
+        cols = pl.ds(k * BATCH * WIDE, BATCH * WIDE)
+        reads.append(pltpu.make_async_copy(w_ref.at[:, cols], w_buf.at[:, cols], in_sem.at[k]))
+        reads[k].start()
+    place_in = pltpu.make_async_copy(place_hbm, place_ref, place_sem)
+    place_in.start()
+    for j in range(PIECE):
+        if j % BATCH == 0:
+            reads[j // BATCH].wait()
+        to_rows(w_buf[:, j * WIDE : (j + 1) * WIDE], j, rows_ref)
+    round_rows(rows_ref, bf_ref)
+    place_in.wait()
+    send_rows(place_ref, bf_ref, all_ref, out_ref, sem)
+    pltpu.make_async_copy(all_ref, out_ref, sem).wait()
 
 
 def pack(place, master):
     return pl.pallas_call(
         pack_kernel,
         out_shape=jax.ShapeDtypeStruct((place.size, PIECE, WIDE), BF16),
-        in_specs=[in_smem, in_hbm],
+        in_specs=[in_hbm] * 2,
         out_specs=in_hbm,
         scratch_shapes=[
             VMEM(master.shape, F32),
             VMEM(ROW_STATE, F32),
             VMEM((EXPERTS, PIECE, WIDE), BF16),
+            VMEM((place.size, PIECE, WIDE), BF16),
+            SMEM(place.shape, jnp.int32),
+            pltpu.SemaphoreType.DMA((PIECE // BATCH,)),
             pltpu.SemaphoreType.DMA,
             pltpu.SemaphoreType.DMA,
         ],
@@ -93,29 +118,14 @@
     )(place, master)
 
 
-def rows_kernel(in_ref, out_ref):
-    for j in range(PIECE):
-        to_rows(in_ref[:, j * WIDE : (j + 1) * WIDE], j, out_ref)
-
-
-def rows_of(values):
-    return pl.pallas_call(
-        rows_kernel,
-        out_shape=jax.ShapeDtypeStruct(ROW_STATE, F32),
-        compiler_params=params(LIMIT),
-        cost_estimate=pl.CostEstimate(flops=values.size, bytes_accessed=8 * values.size, transcendentals=0),
-        name="rows_of",
-    )(values)
-
-
 PARTS = 2
 DEEP = D // PARTS
 TILE = 256
 
 
-def expert_kernel(x_hbm, dy_hbm, w_ref, g_ref, dz_out, *scratch):
+def expert_kernel(step, count_hbm, x_hbm, dy_hbm, w_ref, g_ref, dz_out, *scratch):
     x_ref, dy_ref, dz_ref, wgu_ref, wire_ref, wide_ref, wd_ref = scratch[:7]
-    z_ref, dh_ref, h_ref, ht_ref, g_buf, in_sem, out_sem, dz_sem = scratch[7:]
+    z_ref, dh_ref, h_ref, ht_ref, g_buf, count_ref, in_sem, out_sem, dz_sem = scratch[7:]
     reads = []
 
     def read(source, target):
@@ -124,12 +134,14 @@
         return reads[-1]
 
     down_in = read(w_ref.at[pl.ds(D, 2 * FF), :], wire_ref)
-    dy_in = read(dy_hbm, dy_ref)
-    x_in = read(x_hbm, x_ref)
+    dy_in = read(dy_hbm.at[step], dy_ref)
+    x_in = read(x_hbm.at[step], x_ref)
     parts = []
     for k in range(PARTS):
         rows = pl.ds(k * DEEP, DEEP)
         parts.append(read(w_ref.at[rows, :], wgu_ref.at[rows, :]))
+
+    count_in = read(count_hbm, count_ref)
 
     down_in.wait()
     for t in range(2 * FF // TILE):
@@ -143,6 +155,8 @@
     for n in range(FF // TILE):
         cols = slice(n * TILE, (n + 1) * TILE)
         dh_ref[:, cols] = dot(dy_ref[...], wd_ref[cols, :], NT)
+    count_in.wait()
+    live = lax.broadcasted_iota(jnp.int32, (ROWS, TILE), 0) < count_ref[step]
     x_in.wait()
     for k in range(PARTS):
         parts[k].wait()
@@ -157,11 +171,11 @@
             if k < PARTS - 1:
                 z_ref[:, cols], z_ref[:, ups] = gate, up
                 continue
-            dh = dh_ref[:, cols]
+            dh = jnp.where(live, dh_ref[:, cols], 0.0)
             sig = jax.nn.sigmoid(gate)
             act = gate * sig
             slope = sig * (1.0 + gate * (1.0 - sig))
-            h_ref[:, cols] = (act * up).astype(BF16)
+            h_ref[:, cols] = jnp.where(live, act * up, 0.0).astype(BF16)
             dz_ref[:, cols] = (dh * up * slope).astype(BF16)
             dz_ref[:, ups] = (dh * act).astype(BF16)
     dz_copy = pltpu.make_async_copy(dz_ref, dz_out, dz_sem)
@@ -189,14 +203,14 @@
     dz_copy.wait()
 
 
-def expert(x, dy, weights):
+def expert(step, counts, x, dy, weights):
     return pl.pallas_call(
-        expert_kernel,
+        functools.partial(expert_kernel, step),
         out_shape=(
             jax.ShapeDtypeStruct(weights.shape, BF16),
             jax.ShapeDtypeStruct((ROWS, 2 * FF), BF16),
         ),
-        in_specs=[in_hbm] * 3,
+        in_specs=[in_hbm] * 4,
         out_specs=(in_hbm, in_hbm),
         scratch_shapes=[
             VMEM((ROWS, D), BF16),
@@ -211,13 +225,14 @@
             VMEM((ROWS, FF), BF16),
             VMEM((FF, ROWS), BF16),
             VMEM(weights.shape, BF16),
-            pltpu.SemaphoreType.DMA((PARTS + 3,)),
+            SMEM(counts.shape, jnp.int32),
+            pltpu.SemaphoreType.DMA((PARTS + 4,)),
             pltpu.SemaphoreType.DMA,
             pltpu.SemaphoreType.DMA,
         ],
         compiler_params=params(LIMIT),
         name="expert",
-    )(x, dy, weights)
+    )(counts, x, dy, weights)
 
 
 def row_grad_kernel(dz_ref, w_ref, out_ref):
@@ -247,11 +262,14 @@
     return momentum, curvature, master
 
 
-GROUP = 16
 UNROLL = 2
 
 
-def add_slots(place_ref, in_ref, buf_ref, acc_ref, sems):
+def add_slots(places, place_ref, in_ref, buf_ref, acc_ref, sems):
+    for copy in places:
+        copy.start()
+
+
     def read(k):
         part = pl.ds(k * GROUP, GROUP)
         return pltpu.make_async_copy(in_ref.at[part], buf_ref.at[part], sems.at[k])
@@ -261,6 +279,8 @@
         read(k).start()
     for acc in acc_ref:
         acc[...] = jnp.zeros_like(acc)
+    for copy in places:
+        copy.wait()
 
     @pl.loop(0, groups)
     def _(k):
@@ -281,77 +301,60 @@
     return jnp.concatenate(parts, axis=1)
 
 
-def first_update_kernel(place_ref, next_ref, in_ref, m_ref, c_ref, w_ref, g_ref, out_ref, *scratch):
-    buf_ref, even_ref, odd_ref, bf_ref, m_buf, c_buf, w_buf, sems, state_sem, out_sem, g_sem = scratch
+def first_update_kernel(place_hbm, next_hbm, in_ref, m_ref, c_ref, w_ref, out_ref, *scratch):
+    buf_ref, even_ref, odd_ref, bf_ref, m_buf, c_buf, w_buf = scratch[:7]
+    place_ref, next_ref, place_sem, sems, state_sem, out_sem = scratch[7:]
+    places = [
+        pltpu.make_async_copy(place_hbm, place_ref, place_sem.at[0]),
+        pltpu.make_async_copy(next_hbm, next_ref, place_sem.at[1]),
+    ]
     state = [
         pltpu.make_async_copy(a, b, state_sem.at[i])
         for i, (a, b) in enumerate(((m_ref, m_buf), (c_ref, c_buf), (w_ref, w_buf)))
     ]
     for copy in state:
         copy.start()
-    add_slots(place_ref, in_ref, buf_ref, (even_ref, odd_ref), sems)
+    add_slots(places, place_ref, in_ref, buf_ref, (even_ref, odd_ref), sems)
     for copy in state:
         copy.wait()
 
-    @pl.loop(0, EXPERTS)
-    def _(e):
-        rows = pl.ds(pl.multiple_of(e * PIECE, 8), PIECE)
-        for c in range(WIDE // LANES):
-            grads = (even_ref[c, rows, :] + odd_ref[c, rows, :]) * grad_scale
-            even_ref[c, rows, :] = grads
-            master = sophia(grads, m_buf[c, rows, :], c_buf[c, rows, :], w_buf[c, rows, :])[2]
-            bf_ref[e, :, c * LANES : (c + 1) * LANES] = master.astype(BF16)
-
-    send_rows(next_ref, bf_ref, out_ref, out_sem)
-    g_copy = pltpu.make_async_copy(even_ref, g_ref, g_sem)
-    g_copy.start()
-    pltpu.make_async_copy(out_ref, out_ref, out_sem).wait()
-    g_copy.wait()
+    for j in range(PIECE):
+        cols = slice(j * WIDE, (j + 1) * WIDE)
+        grads = (from_rows(even_ref, j) + from_rows(odd_ref, j)) * grad_scale
+        to_rows(sophia(grads, m_buf[:, cols], c_buf[:, cols], w_buf[:, cols])[2], j, even_ref)
+    round_rows(even_ref, bf_ref)
+    send_rows(next_ref, bf_ref, buf_ref, out_ref, out_sem)
+    pltpu.make_async_copy(buf_ref, out_ref, out_sem).wait()
 
 
 def first_update(place, next_place, arrived, momentum, curvature, master):
     dma = pltpu.SemaphoreType.DMA
     return pl.pallas_call(
         first_update_kernel,
-        out_shape=(jax.ShapeDtypeStruct(ROW_STATE, F32), jax.ShapeDtypeStruct(arrived.shape, BF16)),
-        in_specs=[in_smem] * 2 + [in_hbm] * 4,
-        out_specs=(in_hbm,) * 2,
+        out_shape=jax.ShapeDtypeStruct(arrived.shape, BF16),
+        in_specs=[in_hbm] * 6,
+        out_specs=in_hbm,
         scratch_shapes=[VMEM(arrived.shape, BF16)]
         + [VMEM(ROW_STATE, F32)] * 2
         + [VMEM((EXPERTS, PIECE, WIDE), BF16)]
-        + [VMEM(ROW_STATE, F32)] * 3
-        + [dma((arrived.shape[0] // GROUP,)), dma((3,)), dma, dma],
+        + [VMEM(master.shape, F32)] * 3
+        + [SMEM(place.shape, jnp.int32)] * 2
+        + [dma((2,)), dma((arrived.shape[0] // GROUP,)), dma((3,)), dma],
         compiler_params=params(LIMIT),
         name="first_update",
     )(place, next_place, arrived, momentum, curvature, master)
 
 
-def first_state_kernel(g_ref, m_ref, c_ref, w_ref, mo_ref, co_ref, wo_ref):
-    for j in range(PIECE):
-        cols = slice(j * WIDE, (j + 1) * WIDE)
-        values = sophia(from_rows(g_ref, j), m_ref[:, cols], c_ref[:, cols], w_ref[:, cols])
-        mo_ref[:, cols], co_ref[:, cols], wo_ref[:, cols] = values
-
-
-def first_state(grads, momentum, curvature, master):
-    return pl.pallas_call(
-        first_state_kernel,
-        out_shape=(jax.ShapeDtypeStruct(master.shape, F32),) * 3,
-        compiler_params=params(LIMIT),
-        cost_estimate=pl.CostEstimate(flops=9 * master.size, bytes_accessed=28 * master.size, transcendentals=0),
-        name="first_state",
-    )(grads, momentum, curvature, master)
-
-
-def last_update_kernel(place_ref, in_ref, m_ref, c_ref, w_ref, mo_ref, co_ref, wo_ref, *scratch):
-    buf_ref, even_ref, odd_ref, m_buf, c_buf, w_buf, sems, state_sem, out_sem = scratch
+def full_update_kernel(place_hbm, in_ref, m_ref, c_ref, w_ref, mo_ref, co_ref, wo_ref, *scratch):
+    buf_ref, even_ref, odd_ref, m_buf, c_buf, w_buf, place_ref, place_sem, sems, state_sem, out_sem = scratch
+    places = [pltpu.make_async_copy(place_hbm, place_ref, place_sem)]
     state = [
         pltpu.make_async_copy(a, b, state_sem.at[i])
         for i, (a, b) in enumerate(((m_ref, m_buf), (c_ref, c_buf), (w_ref, w_buf)))
     ]
     for copy in state:
         copy.start()
-    add_slots(place_ref, in_ref, buf_ref, (even_ref, odd_ref), sems)
+    add_slots(places, place_ref, in_ref, buf_ref, (even_ref, odd_ref), sems)
     for copy in state:
         copy.wait()
     for j in range(PIECE):
@@ -365,19 +368,21 @@
         pltpu.make_async_copy(buf, out, out_sem.at[i]).wait()
 
 
-def last_update(place, arrived, momentum, curvature, master):
+def full_update(place, arrived, momentum, curvature, master):
     dma = pltpu.SemaphoreType.DMA
     return pl.pallas_call(
-        last_update_kernel,
+        full_update_kernel,
         out_shape=(jax.ShapeDtypeStruct(master.shape, F32),) * 3,
-        in_specs=[in_smem] + [in_hbm] * 4,
+        in_specs=[in_hbm] * 5,
         out_specs=(in_hbm,) * 3,
         scratch_shapes=[VMEM(arrived.shape, BF16)]
         + [VMEM(ROW_STATE, F32)] * 2
         + [VMEM(master.shape, F32)] * 3
-        + [dma((arrived.shape[0] // GROUP,)), dma((3,)), dma((3,))],
+        + [SMEM(place.shape, jnp.int32)]
+        + [dma, dma((arrived.shape[0] // GROUP,)), dma((3,)), dma((3,))],
         compiler_params=params(LIMIT),
-        name="last_update",
+        cost_estimate=pl.CostEstimate(flops=20 * master.size, bytes_accessed=16 << 20, transcendentals=0),
+        name="full_update",
     )(place, arrived, momentum, curvature, master)
 
 
@@ -387,21 +392,20 @@
 
 def body(token_rows, cotangents, row_counts, old_place, new_place, momentum, curvature, master):
     old_place, new_place = old_place.T, new_place.T
+    x, dy = (v.reshape(-1, ROWS, D) for v in (token_rows, cotangents))
+    counts = row_counts.reshape(-1)
 
     def slots(step, outgoing):
         arrived = exchange(outgoing)
         weights = arrived.reshape(-1, WIDE)
-        live = jnp.arange(ROWS, dtype=jnp.int32)[:, None] < row_counts[step, 0, 0]
-        dy = jnp.where(live, cotangents[step, 0, 0], jnp.zeros((), BF16))
-        grads, dz = expert(token_rows[step, 0, 0], dy, weights)
+        grads, dz = expert(step, counts, x, dy, weights)
         return exchange(grads.reshape(arrived.shape)), row_grad(dz, weights)
 
     arrived, first_rows = slots(0, pack(old_place, master))
-    state = [rows_of(v) for v in (momentum, curvature, master)]
-    grads, outgoing = first_update(old_place, new_place, arrived, *state)
+    outgoing = first_update(old_place, new_place, arrived, momentum, curvature, master)
+    state = full_update(old_place, arrived, momentum, curvature, master)
     arrived, last_rows = slots(1, outgoing)
-    state = first_state(grads, momentum, curvature, master)
-    state = last_update(new_place, arrived, *state)
+    state = full_update(new_place, arrived, *state)
     return (jnp.stack([first_rows, last_rows])[:, None, None], *state)
 
 

time: 375 us -> 370 us (0.987)
  blocking collectives: 80.5 us -> 247 us
  waiting for transfers between devices: 192 us -> 54.8 us
  starting transfers between devices: 23.4 us -> 5.97 us
  Pallas kernels: 66.4 us -> 53.9 us
    all_to_all x1 -> x3, blocking collectives: 80.5 us -> 247 us  [exchange(): return lax.all_to_all(blocks, ('slot', 'grp'), 0, 0, tiled=True)]
    all_to_all x3 -> x1, waiting for transfers between devices: 192 us -> 54.8 us  [exchange(): return lax.all_to_all(blocks, ('slot', 'grp'), 0, 0, tiled=True)]
    all_to_all x3 -> x1, starting transfers between devices: 23.4 us -> 5.97 us  [exchange(): return lax.all_to_all(blocks, ('slot', 'grp'), 0, 0, tiled=True)]
    pallas_call x8 -> x5, Pallas kernels: 51.1 us -> 42.5 us  [the longest x2 20.1 us: expert(): pl.pallas_call(functools.partial(expert_kernel, step), out_shape=(jax.Sha...]
  transfers between devices with their start and end apart: 3 -> 1, of which waited for: 3 -> 1; matrix products, arithmetic and copies ran while one was open for 2% -> 1% of each run, Pallas kernels for 7% -> 4%
where the time goes in v4:
time: 370 us
  blocking collectives  247 us (67%)
  waiting for transfers between devices  54.8 us (15%)
  Pallas kernels  53.9 us (15%)
  starting transfers between devices  5.97 us (2%)
  local copies, waits for them, and re-layouts  5.57 us (2%)
    all_to_all x3, blocking collectives, exchange(): return lax.all_to_all(blocks, ('slot', 'grp'), 0, 0, tiled=True)  247 us
    all_to_all x1, waiting for transfers between devices, exchange(): return lax.all_to_all(blocks, ('slot', 'grp'), 0, 0, tiled=True)  54.8 us
    pallas_call x2, Pallas kernels, expert(): pl.pallas_call(functools.partial(expert_kernel, step), out_shape=(jax.Sha...  20.1 us
    pallas_call x2, Pallas kernels, full_update(): pl.pallas_call(full_update_kernel, out_shape=(jax.ShapeDtypeStruct(master...  13.3 us
    pallas_call x1, Pallas kernels, first_update(): pl.pallas_call(first_update_kernel, out_shape=jax.ShapeDtypeStruct(arrive...  9.11 us
  transfers between devices with their start and end apart: 1, of which 1 were waited for; matrix products, arithmetic and copies ran while one was open for 1% of the time, Pallas kernels for 4%

profile of v4, /device:TPU:0, one launch (start us, length us, event | category | flops | bytes accessed | tf_op | source)
XLA Modules:
  0.0 369.9 jit_solution(1801799169149248051)
XLA Ops:
  0.6 4.4 %pack.1 = bf16[128,24,1024]{2,1,0:T(8,128)(2,1)} custom-call(s32[4,32]{1,0:T(4,128)} %bitcast.27, f32[16,24576]{1,0:T(8,128)} %w_ref.5), custom_call_target="tpu_custom_call" | custom-call | tf_op jit(solution)/shard_map/pack/pallas_call | solution.py:101
  5.1 86.0 %all_to_all.20 = bf16[128,24,1024]{2,1,0:T(8,128)(2,1)} all-to-all(bf16[128,24,1024]{2,1,0:T(8,128)(2,1)} %pack.1), channel_id=1, replica_groups=mesh['slot'=32,'grp'=4] {'slot','grp'}, dimensions={0} | all-to-all | bytes 12582912 | tf_op jit(solution)/shard_map/all_to_all | solution.py:390
  91.1 10.1 %expert.2 = (bf16[3072,1024]{1,0:T(8,128)(2,1)}, bf16[384,1024]{1,0:T(8,128)(2,1)}) custom-call(s32[2]{0:T(128)} %bitcast.32, bf16[2,384,2048]{2,1,0:T(8,128)(2,1)} %bitcast.21, bf16[2,384,2048]{2,1,0:T(8,128)(2,1)} %bitcast.23, bf16[3072,1024]{1,0:T(8,128)(2,1)} %bitcast.17), custom_call_target="tpu_custom_call" | custom-call | tf_op jit(solution)/shard_map/expert/pallas_call | solution.py:207
  101.1 80.5 %all_to_all.21.in_ref = bf16[128,24,1024]{2,1,0:T(8,128)(2,1)} all-to-all(bf16[128,24,1024]{2,1,0:T(8,128)(2,1)} %bitcast.26), channel_id=1, replica_groups=mesh['slot'=32,'grp'=4] {'slot','grp'}, dimensions={0} | all-to-all | bytes 12582912 | tf_op jit(solution)/shard_map/all_to_all | solution.py:390
  181.6 9.1 %first_update.1 = bf16[128,24,1024]{2,1,0:T(8,128)(2,1)} custom-call(s32[4,32]{1,0:T(4,128)} %bitcast.28, s32[4,32]{1,0:T(4,128)} %bitcast.30, bf16[128,24,1024]{2,1,0:T(8,128)(2,1)} %all_to_all.21.in_ref, f32[16,24576]{1,0:T(8,128)} %m_ref.3, f32[16,24576]{1,0:T(8,128)} %c_ref.3, f32[16,24576]{1,0:T(8,128)} %w_ref.5), custom_call_target="tpu_custom_call" | custom-call | tf_op jit(solution)/shard_map/first_update/pallas_call | solution.py:332
  190.7 80.5 %all_to_all.22 = bf16[128,24,1024]{2,1,0:T(8,128)(2,1)} all-to-all(bf16[128,24,1024]{2,1,0:T(8,128)(2,1)} %first_update.1), channel_id=1, replica_groups=mesh['slot'=32,'grp'=4] {'slot','grp'}, dimensions={0} | all-to-all | bytes 12582912 | tf_op jit(solution)/shard_map/all_to_all | solution.py:390
  271.2 10.1 %expert.3 = (bf16[3072,1024]{1,0:T(8,128)(2,1)}, bf16[384,1024]{1,0:T(8,128)(2,1)}) custom-call(s32[2]{0:T(128)} %bitcast.33, bf16[2,384,2048]{2,1,0:T(8,128)(2,1)} %bitcast.22, bf16[2,384,2048]{2,1,0:T(8,128)(2,1)} %bitcast.24, bf16[3072,1024]{1,0:T(8,128)(2,1)} %bitcast.15), custom_call_target="tpu_custom_call" | custom-call | tf_op jit(solution)/shard_map/expert/pallas_call | solution.py:207
  281.2 0.0 copy-start.3
  281.2 6.0 %all-to-all-start.3 = ((bf16[128,24,1024]{2,1,0:T(8,128)(2,1)}), bf16[128,24,1024]{2,1,0:T(8,128)(2,1)}, u32[]{:S(2)}, u32[]{:S(2)}) async-start(bf16[128,24,1024]{2,1,0:T(8,128)(2,1)} %bitcast.25), calls=%async_computation.3 | async-start | bytes 12582912 | tf_op jit(solution)/shard_map/all_to_all | solution.py:390
  287.2 0.0 copy-done.3
  287.2 0.0 copy-start.1
  287.2 2.8 copy-done.1
  290.0 3.5 row_grad.2
  293.5 0.0 copy-start.2
  293.5 6.7 %full_update.2 = (f32[16,24576]{1,0:T(8,128)}, f32[16,24576]{1,0:T(8,128)}, f32[16,24576]{1,0:T(8,128)}) custom-call(s32[4,32]{1,0:T(4,128)} %bitcast.29, bf16[128,24,1024]{2,1,0:T(8,128)(2,1)} %all_to_all.21.in_ref, f32[16,24576]{1,0:T(8,128)} %m_ref.3, f32[16,24576]{1,0:T(8,128)} %c_ref.3, f32[16,24576]{1,0:T(8,128)} %w_ref.5), custom_call_target="tpu_custom_call" | custom-call | flops 7864320 | bytes 16777216 | tf_op jit(solution)/shard_map/full_update/pallas_call | solution.py:373
  300.2 0.0 copy-done.2
  300.2 0.0 copy-start
  300.2 2.8 copy-done
  303.0 3.5 row_grad.3
  306.5 1.9 maximum_bitcast_fusion
  308.4 54.8 %all-to-all-done.3.in_ref = bf16[128,24,1024]{2,1,0:T(8,128)(2,1)} async-done(((bf16[128,24,1024]{2,1,0:T(8,128)(2,1)}), bf16[128,24,1024]{2,1,0:T(8,128)(2,1)}, u32[]{:S(2)}, u32[]{:S(2)}) %all-to-all-start.3) | async-done | bytes 6291488 | tf_op jit(solution)/shard_map/all_to_all | solution.py:390
  363.2 6.6 %full_update.3 = (f32[16,24576]{1,0:T(8,128)}, f32[16,24576]{1,0:T(8,128)}, f32[16,24576]{1,0:T(8,128)}) custom-call(s32[4,32]{1,0:T(4,128)} %bitcast.31, bf16[128,24,1024]{2,1,0:T(8,128)(2,1)} %all-to-all-done.3.in_ref, f32[16,24576]{1,0:T(8,128)} %get-tuple-element.18.m_ref, f32[16,24576]{1,0:T(8,128)} %get-tuple-element.19.c_ref, ...), custom_call_target="tpu_custom_call" | custom-call | flops 7864320 | bytes 16777216 | tf_op jit(solution)/shard_map/full_update/pallas_call | solution.py:373
Async XLA Ops:
  281.2 6.0 %copy-start.3 = (bf16[384,1024]{1,0:T(8,128)(2,1)S(1)}, bf16[384,1024]{1,0:T(8,128)(2,1)}, u32[]{:S(2)}) copy-start(bf16[384,1024]{1,0:T(8,128)(2,1)} %get-tuple-element.14.dz_ref) | copy-start | bytes 2359300
  281.2 81.9 %all-to-all-start.3 = ((bf16[128,24,1024]{2,1,0:T(8,128)(2,1)}), bf16[128,24,1024]{2,1,0:T(8,128)(2,1)}, u32[]{:S(2)}, u32[]{:S(2)}) async-start(bf16[128,24,1024]{2,1,0:T(8,128)(2,1)} %bitcast.25), calls=%async_computation.3 | async-start | bytes 12582912 | tf_op jit(solution)/shard_map/all_to_all | solution.py:390
  287.2 2.8 copy-start.1
  293.5 6.7 %copy-start.2 = (bf16[384,1024]{1,0:T(8,128)(2,1)S(1)}, bf16[384,1024]{1,0:T(8,128)(2,1)}, u32[]{:S(2)}) copy-start(bf16[384,1024]{1,0:T(8,128)(2,1)} %get-tuple-element.16.dz_ref) | copy-start | bytes 2359300
  300.2 2.8 copy-start

commit v5 on v4

--- a/solution.py
+++ b/solution.py
@@ -53,6 +53,7 @@
         rows_ref[c, pl.ds(j, values.shape[0], PIECE), :] = values[:, c * LANES : (c + 1) * LANES]
 
 
+SPAN = 8
 BATCH = 4
 GROUP = 8
 
@@ -265,7 +266,16 @@
 UNROLL = 2
 
 
-def add_slots(places, place_ref, in_ref, buf_ref, acc_ref, sems):
+def state_reads(pairs, sems):
+    copies = []
+    for k in range(PIECE // SPAN):
+        cols = pl.ds(k * SPAN * WIDE, SPAN * WIDE)
+        for i, (source, target) in enumerate(pairs):
+            copies.append(pltpu.make_async_copy(source.at[:, cols], target.at[:, cols], sems.at[3 * k + i]))
+    return copies
+
+
+def add_slots(places, state, place_ref, in_ref, buf_ref, acc_ref, sems):
     for copy in places:
         copy.start()
 
@@ -277,6 +287,8 @@
     groups = buf_ref.shape[0] // GROUP
     for k in range(groups):
         read(k).start()
+    for copy in state:
+        copy.start()
     for acc in acc_ref:
         acc[...] = jnp.zeros_like(acc)
     for copy in places:
@@ -308,18 +320,14 @@
         pltpu.make_async_copy(place_hbm, place_ref, place_sem.at[0]),
         pltpu.make_async_copy(next_hbm, next_ref, place_sem.at[1]),
     ]
-    state = [
-        pltpu.make_async_copy(a, b, state_sem.at[i])
-        for i, (a, b) in enumerate(((m_ref, m_buf), (c_ref, c_buf), (w_ref, w_buf)))
-    ]
-    for copy in state:
-        copy.start()
-    add_slots(places, place_ref, in_ref, buf_ref, (even_ref, odd_ref), sems)
-    for copy in state:
-        copy.wait()
+    state = state_reads(((m_ref, m_buf), (c_ref, c_buf), (w_ref, w_buf)), state_sem)
+    add_slots(places, state, place_ref, in_ref, buf_ref, (even_ref, odd_ref), sems)
 
     for j in range(PIECE):
         cols = slice(j * WIDE, (j + 1) * WIDE)
+        if j % SPAN == 0:
+            for copy in state[3 * j // SPAN : 3 * j // SPAN + 3]:
+                copy.wait()
         grads = (from_rows(even_ref, j) + from_rows(odd_ref, j)) * grad_scale
         to_rows(sophia(grads, m_buf[:, cols], c_buf[:, cols], w_buf[:, cols])[2], j, even_ref)
     round_rows(even_ref, bf_ref)
@@ -339,7 +347,7 @@
         + [VMEM((EXPERTS, PIECE, WIDE), BF16)]
         + [VMEM(master.shape, F32)] * 3
         + [SMEM(place.shape, jnp.int32)] * 2
-        + [dma((2,)), dma((arrived.shape[0] // GROUP,)), dma((3,)), dma],
+        + [dma((2,)), dma((arrived.shape[0] // GROUP,)), dma((3 * PIECE // SPAN,)), dma],
         compiler_params=params(LIMIT),
         name="first_update",
     )(place, next_place, arrived, momentum, curvature, master)
@@ -348,17 +356,13 @@
 def full_update_kernel(place_hbm, in_ref, m_ref, c_ref, w_ref, mo_ref, co_ref, wo_ref, *scratch):
     buf_ref, even_ref, odd_ref, m_buf, c_buf, w_buf, place_ref, place_sem, sems, state_sem, out_sem = scratch
     places = [pltpu.make_async_copy(place_hbm, place_ref, place_sem)]
-    state = [
-        pltpu.make_async_copy(a, b, state_sem.at[i])
-        for i, (a, b) in enumerate(((m_ref, m_buf), (c_ref, c_buf), (w_ref, w_buf)))
-    ]
-    for copy in state:
-        copy.start()
-    add_slots(places, place_ref, in_ref, buf_ref, (even_ref, odd_ref), sems)
-    for copy in state:
-        copy.wait()
+    state = state_reads(((m_ref, m_buf), (c_ref, c_buf), (w_ref, w_buf)), state_sem)
+    add_slots(places, state, place_ref, in_ref, buf_ref, (even_ref, odd_ref), sems)
     for j in range(PIECE):
         cols = slice(j * WIDE, (j + 1) * WIDE)
+        if j % SPAN == 0:
+            for copy in state[3 * j // SPAN : 3 * j // SPAN + 3]:
+                copy.wait()
         grads = (from_rows(even_ref, j) + from_rows(odd_ref, j)) * grad_scale
         values = sophia(grads, m_buf[:, cols], c_buf[:, cols], w_buf[:, cols])
         for i, (buf, out) in enumerate(((m_buf, mo_ref), (c_buf, co_ref), (w_buf, wo_ref))):
@@ -379,7 +383,7 @@
         + [VMEM(ROW_STATE, F32)] * 2
         + [VMEM(master.shape, F32)] * 3
         + [SMEM(place.shape, jnp.int32)]
-        + [dma, dma((arrived.shape[0] // GROUP,)), dma((3,)), dma((3,))],
+        + [dma, dma((arrived.shape[0] // GROUP,)), dma((3 * PIECE // SPAN,)), dma((3,))],
         compiler_params=params(LIMIT),
         cost_estimate=pl.CostEstimate(flops=20 * master.size, bytes_accessed=16 << 20, transcendentals=0),
         name="full_update",

time: 370 us -> 370 us (level)
  no operation moved by 1% of the time
where the time goes in v5:
time: 370 us; the launch traced here: 369 us
  blocking collectives  247 us (67%)
  waiting for transfers between devices  54.9 us (15%)
  Pallas kernels  53.1 us (14%)
  starting transfers between devices  5.97 us (2%)
  local copies, waits for them, and re-layouts  5.57 us (2%)
    all_to_all x3, blocking collectives, exchange(): return lax.all_to_all(blocks, ('slot', 'grp'), 0, 0, tiled=True)  247 us
    all_to_all x1, waiting for transfers between devices, exchange(): return lax.all_to_all(blocks, ('slot', 'grp'), 0, 0, tiled=True)  54.9 us
    pallas_call x2, Pallas kernels, expert(): pl.pallas_call(functools.partial(expert_kernel, step), out_shape=(jax.Sha...  20.1 us
    pallas_call x2, Pallas kernels, full_update(): pl.pallas_call(full_update_kernel, out_shape=(jax.ShapeDtypeStruct(master...  13.1 us
    pallas_call x1, Pallas kernels, first_update(): pl.pallas_call(first_update_kernel, out_shape=jax.ShapeDtypeStruct(arrive...  8.56 us
  transfers between devices with their start and end apart: 1, of which 1 were waited for; matrix products, arithmetic and copies ran while one was open for 1% of the time, Pallas kernels for 4%

profile of v5, /device:TPU:0, one launch (start us, length us, event | category | flops | bytes accessed | tf_op | source)
XLA Modules:
  0.0 369.3 jit_solution(18300639713991026927)
XLA Ops:
  0.6 4.4 %pack.1 = bf16[128,24,1024]{2,1,0:T(8,128)(2,1)} custom-call(s32[4,32]{1,0:T(4,128)} %bitcast.27, f32[16,24576]{1,0:T(8,128)} %w_ref.5), custom_call_target="tpu_custom_call" | custom-call | tf_op jit(solution)/shard_map/pack/pallas_call | solution.py:102
  5.1 86.0 %all_to_all.20 = bf16[128,24,1024]{2,1,0:T(8,128)(2,1)} all-to-all(bf16[128,24,1024]{2,1,0:T(8,128)(2,1)} %pack.1), channel_id=1, replica_groups=mesh['slot'=32,'grp'=4] {'slot','grp'}, dimensions={0} | all-to-all | bytes 12582912 | tf_op jit(solution)/shard_map/all_to_all | solution.py:394
  91.1 10.1 %expert.2 = (bf16[3072,1024]{1,0:T(8,128)(2,1)}, bf16[384,1024]{1,0:T(8,128)(2,1)}) custom-call(s32[2]{0:T(128)} %bitcast.32, bf16[2,384,2048]{2,1,0:T(8,128)(2,1)} %bitcast.21, bf16[2,384,2048]{2,1,0:T(8,128)(2,1)} %bitcast.23, bf16[3072,1024]{1,0:T(8,128)(2,1)} %bitcast.17), custom_call_target="tpu_custom_call" | custom-call | tf_op jit(solution)/shard_map/expert/pallas_call | solution.py:208
  101.1 80.5 %all_to_all.21.in_ref = bf16[128,24,1024]{2,1,0:T(8,128)(2,1)} all-to-all(bf16[128,24,1024]{2,1,0:T(8,128)(2,1)} %bitcast.26), channel_id=1, replica_groups=mesh['slot'=32,'grp'=4] {'slot','grp'}, dimensions={0} | all-to-all | bytes 12582912 | tf_op jit(solution)/shard_map/all_to_all | solution.py:394
  181.6 8.6 %first_update.1 = bf16[128,24,1024]{2,1,0:T(8,128)(2,1)} custom-call(s32[4,32]{1,0:T(4,128)} %bitcast.28, s32[4,32]{1,0:T(4,128)} %bitcast.30, bf16[128,24,1024]{2,1,0:T(8,128)(2,1)} %all_to_all.21.in_ref, f32[16,24576]{1,0:T(8,128)} %m_ref.3, f32[16,24576]{1,0:T(8,128)} %c_ref.3, f32[16,24576]{1,0:T(8,128)} %w_ref.5), custom_call_target="tpu_custom_call" | custom-call | tf_op jit(solution)/shard_map/first_update/pallas_call | solution.py:340
  190.2 80.5 %all_to_all.22 = bf16[128,24,1024]{2,1,0:T(8,128)(2,1)} all-to-all(bf16[128,24,1024]{2,1,0:T(8,128)(2,1)} %first_update.1), channel_id=1, replica_groups=mesh['slot'=32,'grp'=4] {'slot','grp'}, dimensions={0} | all-to-all | bytes 12582912 | tf_op jit(solution)/shard_map/all_to_all | solution.py:394
  270.6 10.1 %expert.3 = (bf16[3072,1024]{1,0:T(8,128)(2,1)}, bf16[384,1024]{1,0:T(8,128)(2,1)}) custom-call(s32[2]{0:T(128)} %bitcast.33, bf16[2,384,2048]{2,1,0:T(8,128)(2,1)} %bitcast.22, bf16[2,384,2048]{2,1,0:T(8,128)(2,1)} %bitcast.24, bf16[3072,1024]{1,0:T(8,128)(2,1)} %bitcast.15), custom_call_target="tpu_custom_call" | custom-call | tf_op jit(solution)/shard_map/expert/pallas_call | solution.py:208
  280.7 0.0 copy-start.3
  280.7 6.0 %all-to-all-start.3 = ((bf16[128,24,1024]{2,1,0:T(8,128)(2,1)}), bf16[128,24,1024]{2,1,0:T(8,128)(2,1)}, u32[]{:S(2)}, u32[]{:S(2)}) async-start(bf16[128,24,1024]{2,1,0:T(8,128)(2,1)} %bitcast.25), calls=%async_computation.3 | async-start | bytes 12582912 | tf_op jit(solution)/shard_map/all_to_all | solution.py:394
  286.7 0.0 copy-done.3
  286.7 0.0 copy-start.1
  286.7 2.8 copy-done.1
  289.5 3.5 row_grad.2
  293.0 0.0 copy-start.2
  293.0 6.6 %full_update.2 = (f32[16,24576]{1,0:T(8,128)}, f32[16,24576]{1,0:T(8,128)}, f32[16,24576]{1,0:T(8,128)}) custom-call(s32[4,32]{1,0:T(4,128)} %bitcast.29, bf16[128,24,1024]{2,1,0:T(8,128)(2,1)} %all_to_all.21.in_ref, f32[16,24576]{1,0:T(8,128)} %m_ref.3, f32[16,24576]{1,0:T(8,128)} %c_ref.3, f32[16,24576]{1,0:T(8,128)} %w_ref.5), custom_call_target="tpu_custom_call" | custom-call | flops 7864320 | bytes 16777216 | tf_op jit(solution)/shard_map/full_update/pallas_call | solution.py:377
  299.6 0.0 copy-done.2
  299.6 0.0 copy-start
  299.6 2.8 copy-done
  302.4 3.5 row_grad.3
  305.8 1.9 maximum_bitcast_fusion
  307.8 54.9 %all-to-all-done.3.in_ref = bf16[128,24,1024]{2,1,0:T(8,128)(2,1)} async-done(((bf16[128,24,1024]{2,1,0:T(8,128)(2,1)}), bf16[128,24,1024]{2,1,0:T(8,128)(2,1)}, u32[]{:S(2)}, u32[]{:S(2)}) %all-to-all-start.3) | async-done | bytes 6291488 | tf_op jit(solution)/shard_map/all_to_all | solution.py:394
  362.6 6.5 %full_update.3 = (f32[16,24576]{1,0:T(8,128)}, f32[16,24576]{1,0:T(8,128)}, f32[16,24576]{1,0:T(8,128)}) custom-call(s32[4,32]{1,0:T(4,128)} %bitcast.31, bf16[128,24,1024]{2,1,0:T(8,128)(2,1)} %all-to-all-done.3.in_ref, f32[16,24576]{1,0:T(8,128)} %get-tuple-element.18.m_ref, f32[16,24576]{1,0:T(8,128)} %get-tuple-element.19.c_ref, ...), custom_call_target="tpu_custom_call" | custom-call | flops 7864320 | bytes 16777216 | tf_op jit(solution)/shard_map/full_update/pallas_call | solution.py:377
Async XLA Ops:
  280.7 6.0 %copy-start.3 = (bf16[384,1024]{1,0:T(8,128)(2,1)S(1)}, bf16[384,1024]{1,0:T(8,128)(2,1)}, u32[]{:S(2)}) copy-start(bf16[384,1024]{1,0:T(8,128)(2,1)} %get-tuple-element.14.dz_ref) | copy-start | bytes 2359300
  280.7 81.9 %all-to-all-start.3 = ((bf16[128,24,1024]{2,1,0:T(8,128)(2,1)}), bf16[128,24,1024]{2,1,0:T(8,128)(2,1)}, u32[]{:S(2)}, u32[]{:S(2)}) async-start(bf16[128,24,1024]{2,1,0:T(8,128)(2,1)} %bitcast.25), calls=%async_computation.3 | async-start | bytes 12582912 | tf_op jit(solution)/shard_map/all_to_all | solution.py:394
  286.7 2.8 copy-start.1
  293.0 6.6 %copy-start.2 = (bf16[384,1024]{1,0:T(8,128)(2,1)S(1)}, bf16[384,1024]{1,0:T(8,128)(2,1)}, u32[]{:S(2)}) copy-start(bf16[384,1024]{1,0:T(8,128)(2,1)} %get-tuple-element.16.dz_ref) | copy-start | bytes 2359300
  299.6 2.8 copy-start

commit v6 on v5

--- a/solution.py
+++ b/solution.py
@@ -54,6 +54,7 @@
 
 
 SPAN = 8
+LAST_SPAN = 12
 BATCH = 4
 GROUP = 8
 
@@ -266,10 +267,10 @@
 UNROLL = 2
 
 
-def state_reads(pairs, sems):
+def state_reads(pairs, sems, span):
     copies = []
-    for k in range(PIECE // SPAN):
-        cols = pl.ds(k * SPAN * WIDE, SPAN * WIDE)
+    for k in range(PIECE // span):
+        cols = pl.ds(k * span * WIDE, span * WIDE)
         for i, (source, target) in enumerate(pairs):
             copies.append(pltpu.make_async_copy(source.at[:, cols], target.at[:, cols], sems.at[3 * k + i]))
     return copies
@@ -320,7 +321,7 @@
         pltpu.make_async_copy(place_hbm, place_ref, place_sem.at[0]),
         pltpu.make_async_copy(next_hbm, next_ref, place_sem.at[1]),
     ]
-    state = state_reads(((m_ref, m_buf), (c_ref, c_buf), (w_ref, w_buf)), state_sem)
+    state = state_reads(((m_ref, m_buf), (c_ref, c_buf), (w_ref, w_buf)), state_sem, SPAN)
     add_slots(places, state, place_ref, in_ref, buf_ref, (even_ref, odd_ref), sems)
 
     for j in range(PIECE):
@@ -356,12 +357,12 @@
 def full_update_kernel(place_hbm, in_ref, m_ref, c_ref, w_ref, mo_ref, co_ref, wo_ref, *scratch):
     buf_ref, even_ref, odd_ref, m_buf, c_buf, w_buf, place_ref, place_sem, sems, state_sem, out_sem = scratch
     places = [pltpu.make_async_copy(place_hbm, place_ref, place_sem)]
-    state = state_reads(((m_ref, m_buf), (c_ref, c_buf), (w_ref, w_buf)), state_sem)
+    state = state_reads(((m_ref, m_buf), (c_ref, c_buf), (w_ref, w_buf)), state_sem, LAST_SPAN)
     add_slots(places, state, place_ref, in_ref, buf_ref, (even_ref, odd_ref), sems)
     for j in range(PIECE):
         cols = slice(j * WIDE, (j + 1) * WIDE)
-        if j % SPAN == 0:
-            for copy in state[3 * j // SPAN : 3 * j // SPAN + 3]:
+        if j % LAST_SPAN == 0:
+            for copy in state[3 * j // LAST_SPAN : 3 * j // LAST_SPAN + 3]:
                 copy.wait()
         grads = (from_rows(even_ref, j) + from_rows(odd_ref, j)) * grad_scale
         values = sophia(grads, m_buf[:, cols], c_buf[:, cols], w_buf[:, cols])
@@ -383,7 +384,7 @@
         + [VMEM(ROW_STATE, F32)] * 2
         + [VMEM(master.shape, F32)] * 3
         + [SMEM(place.shape, jnp.int32)]
-        + [dma, dma((arrived.shape[0] // GROUP,)), dma((3 * PIECE // SPAN,)), dma((3,))],
+        + [dma, dma((arrived.shape[0] // GROUP,)), dma((3 * PIECE // LAST_SPAN,)), dma((3,))],
         compiler_params=params(LIMIT),
         cost_estimate=pl.CostEstimate(flops=20 * master.size, bytes_accessed=16 << 20, transcendentals=0),
         name="full_update",

time: 370 us -> 370 us (level)
  no operation moved by 1% of the time
where the time goes in v6:
time: 370 us; the launch traced here: 369 us
  blocking collectives  247 us (67%)
  waiting for transfers between devices  55 us (15%)
  Pallas kernels  52.9 us (14%)
  starting transfers between devices  5.97 us (2%)
  local copies, waits for them, and re-layouts  5.57 us (2%)
    all_to_all x3, blocking collectives, exchange(): return lax.all_to_all(blocks, ('slot', 'grp'), 0, 0, tiled=True)  247 us
    all_to_all x1, waiting for transfers between devices, exchange(): return lax.all_to_all(blocks, ('slot', 'grp'), 0, 0, tiled=True)  55 us
    pallas_call x2, Pallas kernels, expert(): pl.pallas_call(functools.partial(expert_kernel, step), out_shape=(jax.Sha...  20.1 us
    pallas_call x2, Pallas kernels, full_update(): pl.pallas_call(full_update_kernel, out_shape=(jax.ShapeDtypeStruct(master...  12.9 us
    pallas_call x1, Pallas kernels, first_update(): pl.pallas_call(first_update_kernel, out_shape=jax.ShapeDtypeStruct(arrive...  8.56 us
  transfers between devices with their start and end apart: 1, of which 1 were waited for; matrix products, arithmetic and copies ran while one was open for 1% of the time, Pallas kernels for 4%

profile of v6, /device:TPU:0, one launch (start us, length us, event | category | flops | bytes accessed | tf_op | source)
XLA Modules:
  0.0 369.2 jit_solution(12176956114213226066)
XLA Ops:
  0.6 4.4 %pack.1 = bf16[128,24,1024]{2,1,0:T(8,128)(2,1)} custom-call(s32[4,32]{1,0:T(4,128)} %bitcast.27, f32[16,24576]{1,0:T(8,128)} %w_ref.5), custom_call_target="tpu_custom_call" | custom-call | tf_op jit(solution)/shard_map/pack/pallas_call | solution.py:103
  5.1 86.0 %all_to_all.20 = bf16[128,24,1024]{2,1,0:T(8,128)(2,1)} all-to-all(bf16[128,24,1024]{2,1,0:T(8,128)(2,1)} %pack.1), channel_id=1, replica_groups=mesh['slot'=32,'grp'=4] {'slot','grp'}, dimensions={0} | all-to-all | bytes 12582912 | tf_op jit(solution)/shard_map/all_to_all | solution.py:395
  91.1 10.1 %expert.2 = (bf16[3072,1024]{1,0:T(8,128)(2,1)}, bf16[384,1024]{1,0:T(8,128)(2,1)}) custom-call(s32[2]{0:T(128)} %bitcast.32, bf16[2,384,2048]{2,1,0:T(8,128)(2,1)} %bitcast.21, bf16[2,384,2048]{2,1,0:T(8,128)(2,1)} %bitcast.23, bf16[3072,1024]{1,0:T(8,128)(2,1)} %bitcast.17), custom_call_target="tpu_custom_call" | custom-call | tf_op jit(solution)/shard_map/expert/pallas_call | solution.py:209
  101.1 80.5 %all_to_all.21.in_ref = bf16[128,24,1024]{2,1,0:T(8,128)(2,1)} all-to-all(bf16[128,24,1024]{2,1,0:T(8,128)(2,1)} %bitcast.26), channel_id=1, replica_groups=mesh['slot'=32,'grp'=4] {'slot','grp'}, dimensions={0} | all-to-all | bytes 12582912 | tf_op jit(solution)/shard_map/all_to_all | solution.py:395
  181.6 8.6 %first_update.1 = bf16[128,24,1024]{2,1,0:T(8,128)(2,1)} custom-call(s32[4,32]{1,0:T(4,128)} %bitcast.28, s32[4,32]{1,0:T(4,128)} %bitcast.30, bf16[128,24,1024]{2,1,0:T(8,128)(2,1)} %all_to_all.21.in_ref, f32[16,24576]{1,0:T(8,128)} %m_ref.3, f32[16,24576]{1,0:T(8,128)} %c_ref.3, f32[16,24576]{1,0:T(8,128)} %w_ref.5), custom_call_target="tpu_custom_call" | custom-call | tf_op jit(solution)/shard_map/first_update/pallas_call | solution.py:341
  190.2 80.5 %all_to_all.22 = bf16[128,24,1024]{2,1,0:T(8,128)(2,1)} all-to-all(bf16[128,24,1024]{2,1,0:T(8,128)(2,1)} %first_update.1), channel_id=1, replica_groups=mesh['slot'=32,'grp'=4] {'slot','grp'}, dimensions={0} | all-to-all | bytes 12582912 | tf_op jit(solution)/shard_map/all_to_all | solution.py:395
  270.6 10.1 %expert.3 = (bf16[3072,1024]{1,0:T(8,128)(2,1)}, bf16[384,1024]{1,0:T(8,128)(2,1)}) custom-call(s32[2]{0:T(128)} %bitcast.33, bf16[2,384,2048]{2,1,0:T(8,128)(2,1)} %bitcast.22, bf16[2,384,2048]{2,1,0:T(8,128)(2,1)} %bitcast.24, bf16[3072,1024]{1,0:T(8,128)(2,1)} %bitcast.15), custom_call_target="tpu_custom_call" | custom-call | tf_op jit(solution)/shard_map/expert/pallas_call | solution.py:209
  280.7 0.0 copy-start.3
  280.7 6.0 %all-to-all-start.3 = ((bf16[128,24,1024]{2,1,0:T(8,128)(2,1)}), bf16[128,24,1024]{2,1,0:T(8,128)(2,1)}, u32[]{:S(2)}, u32[]{:S(2)}) async-start(bf16[128,24,1024]{2,1,0:T(8,128)(2,1)} %bitcast.25), calls=%async_computation.3 | async-start | bytes 12582912 | tf_op jit(solution)/shard_map/all_to_all | solution.py:395
  286.7 0.0 copy-done.3
  286.7 0.0 copy-start.1
  286.7 2.8 copy-done.1
  289.5 3.5 row_grad.2
  292.9 0.0 copy-start.2
  293.0 6.5 %full_update.2 = (f32[16,24576]{1,0:T(8,128)}, f32[16,24576]{1,0:T(8,128)}, f32[16,24576]{1,0:T(8,128)}) custom-call(s32[4,32]{1,0:T(4,128)} %bitcast.29, bf16[128,24,1024]{2,1,0:T(8,128)(2,1)} %all_to_all.21.in_ref, f32[16,24576]{1,0:T(8,128)} %m_ref.3, f32[16,24576]{1,0:T(8,128)} %c_ref.3, f32[16,24576]{1,0:T(8,128)} %w_ref.5), custom_call_target="tpu_custom_call" | custom-call | flops 7864320 | bytes 16777216 | tf_op jit(solution)/shard_map/full_update/pallas_call | solution.py:378
  299.5 0.0 copy-done.2
  299.5 0.0 copy-start
  299.5 2.8 copy-done
  302.3 3.5 row_grad.3
  305.7 1.9 maximum_bitcast_fusion
  307.7 55.0 %all-to-all-done.3.in_ref = bf16[128,24,1024]{2,1,0:T(8,128)(2,1)} async-done(((bf16[128,24,1024]{2,1,0:T(8,128)(2,1)}), bf16[128,24,1024]{2,1,0:T(8,128)(2,1)}, u32[]{:S(2)}, u32[]{:S(2)}) %all-to-all-start.3) | async-done | bytes 6291488 | tf_op jit(solution)/shard_map/all_to_all | solution.py:395
  362.6 6.4 %full_update.3 = (f32[16,24576]{1,0:T(8,128)}, f32[16,24576]{1,0:T(8,128)}, f32[16,24576]{1,0:T(8,128)}) custom-call(s32[4,32]{1,0:T(4,128)} %bitcast.31, bf16[128,24,1024]{2,1,0:T(8,128)(2,1)} %all-to-all-done.3.in_ref, f32[16,24576]{1,0:T(8,128)} %get-tuple-element.18.m_ref, f32[16,24576]{1,0:T(8,128)} %get-tuple-element.19.c_ref, ...), custom_call_target="tpu_custom_call" | custom-call | flops 7864320 | bytes 16777216 | tf_op jit(solution)/shard_map/full_update/pallas_call | solution.py:378
Async XLA Ops:
  280.7 6.0 %copy-start.3 = (bf16[384,1024]{1,0:T(8,128)(2,1)S(1)}, bf16[384,1024]{1,0:T(8,128)(2,1)}, u32[]{:S(2)}) copy-start(bf16[384,1024]{1,0:T(8,128)(2,1)} %get-tuple-element.14.dz_ref) | copy-start | bytes 2359300
  280.7 81.9 %all-to-all-start.3 = ((bf16[128,24,1024]{2,1,0:T(8,128)(2,1)}), bf16[128,24,1024]{2,1,0:T(8,128)(2,1)}, u32[]{:S(2)}, u32[]{:S(2)}) async-start(bf16[128,24,1024]{2,1,0:T(8,128)(2,1)} %bitcast.25), calls=%async_computation.3 | async-start | bytes 12582912 | tf_op jit(solution)/shard_map/all_to_all | solution.py:395
  286.7 2.8 copy-start.1
  292.9 6.5 %copy-start.2 = (bf16[384,1024]{1,0:T(8,128)(2,1)S(1)}, bf16[384,1024]{1,0:T(8,128)(2,1)}, u32[]{:S(2)}) copy-start(bf16[384,1024]{1,0:T(8,128)(2,1)} %get-tuple-element.16.dz_ref) | copy-start | bytes 2359300
  299.5 2.8 copy-start
